TPU v7x, 32 devices: a whole 2x2x4 slice. The times are simulated.
32 devices in a mesh: rows: 8 (over z, y), feat: 4 (over x, core).
Axes of the slice: x: 2, y: 2, z: 4, core: 2. Of those that a mesh axis runs over, the one named last changes fastest.
Arguments:
- bin_codes: int32 [16, 122880], P(None, 'rows'), may hold values from 0 to 255
- node_ids: int32 [122880], P('rows'), may hold values from 0 to 7, as said below
- labels: float32 [122880], P('rows'), may hold values from -1 to 1, as said below
- weights: float32 [122880], P('rows'), as said below
- predictions: float32 [122880], P('rows'), may hold values from -6 to 6
- level3_feature: int32 [8], replicated, may hold values from 0 to 15
- level3_bin: int32 [8], replicated, may hold values from 64 to 191
- level4_feature: int32 [16], replicated, may hold values from 0 to 15
- level4_bin: int32 [16], replicated, may hold values from 64 to 191
Outputs:
- level3_hist: float32 [16, 16, 256], P('feat')
- level4_hist: float32 [16, 32, 256], P('feat')
- leaf_values: float32 [32], replicated
- new_predictions: float32 [122880], P('rows')
- new_weights: float32 [122880], P('rows')
Inputs may be any that keep to these rules, and one draw needn't show every extreme that they name: `node_ids`: node ids of level 3. `labels`: every label is -1 or 1. `weights`: every weight is positive.
All inputs are finite; a program needn't handle non-finite values.
Results may differ from a plain program's by a relative error of at most 0.0003.
Values sent between devices are 32-bit elements; how exact they have to be, the bound alone decides.
No kernel may reach another device: no remote copies, remote signals or barrier semaphores. Data moves between devices by JAX's collectives and lax.ppermute only.
A program may use at most 64 MiB of HBM per device.

v0:
```python
import math

import jax
import jax.numpy as jnp
from jax import lax
from jax.sharding import PartitionSpec as P

FEATURES = 16
BINS = 256


def routing(bin_codes, node_of, features, thresholds):
    node_count = features.shape[0]
    member = node_of[:, None] == jnp.arange(node_count, dtype=jnp.int32)[None, :]
    chosen = jnp.sum(jnp.where(member, features[None, :], 0), axis=1)
    cutoff = jnp.sum(jnp.where(member, thresholds[None, :], 0), axis=1)
    all_ids = jnp.arange(bin_codes.shape[0], dtype=jnp.int32)
    owner_mask = chosen[None, :] == all_ids[:, None]
    picked = jnp.sum(jnp.where(owner_mask, bin_codes, 0), axis=0)
    return (picked > cutoff).astype(jnp.int32)


def partial_histogram(bin_codes, node_of, node_count, weight_bf, signed_bf):
    feature_local = bin_codes.shape[0]
    row_count = node_of.shape[0]
    block_rows = math.gcd(row_count, 1024)
    turns = row_count // block_rows
    code_blocks = bin_codes.reshape(feature_local, turns, block_rows).transpose(1, 0, 2)
    node_blocks = node_of.reshape(turns, block_rows)
    weight_blocks = weight_bf.reshape(turns, block_rows)
    signed_blocks = signed_bf.reshape(turns, block_rows)
    bin_range = jnp.arange(BINS, dtype=jnp.int32)
    node_range = jnp.arange(node_count, dtype=jnp.int32)

    def accumulate(running, pieces):
        code_piece, node_piece, weight_piece, signed_piece = pieces
        member = node_piece[:, None] == node_range[None, :]
        nothing = jnp.zeros((), jnp.bfloat16)
        row_matrix = jnp.concatenate(
            [
                jnp.where(member, weight_piece[:, None], nothing),
                jnp.where(member, signed_piece[:, None], nothing),
            ],
            axis=1,
        )
        onehot_bins = (code_piece[:, :, None] == bin_range[None, None, :]).astype(jnp.bfloat16)
        return (
            running
            + jnp.einsum(
                "rn,frb->fnb", row_matrix, onehot_bins, preferred_element_type=jnp.float32
            ),
            None,
        )

    initial = jnp.zeros((feature_local, 2 * node_count, BINS), jnp.float32)
    running, _ = lax.scan(
        accumulate, initial, (code_blocks, node_blocks, weight_blocks, signed_blocks)
    )
    return running


def combine_rows(partial_value):
    return lax.psum(partial_value, "rows")


def on_device(
    bin_codes,
    node_ids,
    labels,
    weights,
    predictions,
    level3_feature,
    level3_bin,
    level4_feature,
    level4_bin,
):
    feature_local = FEATURES // lax.axis_size("feat")
    feat_position = lax.axis_index("feat")
    feature_base = feat_position * feature_local
    own_codes = lax.dynamic_slice_in_dim(bin_codes, feature_base, feature_local, 0)
    weight_bf = weights.astype(jnp.bfloat16)
    signed_bf = (weights * labels).astype(jnp.bfloat16)
    parents = level3_feature.shape[0]
    parent_partial = partial_histogram(own_codes, node_ids, parents, weight_bf, signed_bf)
    go_three = routing(bin_codes, node_ids, level3_feature, level3_bin)
    node_four = 2 * node_ids + go_three
    second_nodes = jnp.where(go_three == 0, node_ids, -1)
    child_partial = partial_histogram(own_codes, second_nodes, parents, weight_bf, signed_bf)
    level3_hist = combine_rows(parent_partial)
    child_hist = combine_rows(child_partial)
    right_hist = level3_hist - child_hist
    weight_part = jnp.stack([child_hist[:, :parents], right_hist[:, :parents]], axis=2).reshape(
        feature_local, 2 * parents, BINS
    )
    signed_part = jnp.stack([child_hist[:, parents:], right_hist[:, parents:]], axis=2).reshape(
        feature_local, 2 * parents, BINS
    )
    level4_hist = jnp.concatenate([weight_part, signed_part], axis=1)
    go_four = routing(bin_codes, node_four, level4_feature, level4_bin)
    leaf_of = 2 * node_four + go_four
    nodes_four = level4_feature.shape[0]
    leaf_count = 2 * nodes_four
    leaf_member = (leaf_of[:, None] == jnp.arange(leaf_count, dtype=jnp.int32)[None, :]).astype(
        jnp.bfloat16
    )
    paired_rows = jnp.stack([weight_bf, signed_bf], axis=1)
    local_sums = lax.dot_general(
        paired_rows, leaf_member, (((0,), (0,)), ((), ())), preferred_element_type=jnp.float32
    )
    leaf_weight, leaf_signed = lax.psum((local_sums[0], local_sums[1]), "rows")
    leaf_values = leaf_signed / (leaf_weight + 1.0)
    leaf_match = leaf_of[:, None] == jnp.arange(leaf_count, dtype=jnp.int32)[None, :]
    stepped = jnp.sum(jnp.where(leaf_match, leaf_values[None, :], 0.0), axis=1)
    new_predictions = predictions + stepped
    raw_weights = weights * jnp.exp(-labels * stepped)
    grand_sum = lax.psum(jnp.sum(raw_weights), "rows")
    new_weights = raw_weights * (raw_weights.shape[0] * lax.axis_size("rows") / grand_sum)
    return (level3_hist, level4_hist, leaf_values, new_predictions, new_weights)


def solution(mesh):
    placed = (P(None, "rows"), P("rows"), P("rows"), P("rows"), P("rows"), P(), P(), P(), P())
    return jax.shard_map(
        on_device,
        mesh=mesh,
        in_specs=placed,
        out_specs=(P("feat", None, None), P("feat", None, None), P(), P("rows"), P("rows")),
        check_vma=False,
    )
```

profile of v0, /device:TPU:0, one launch (start us, length us, event | category | flops | bytes accessed | tf_op | source)
XLA Modules:
  0.0 162.0 jit_solution(2438244070425970742)
XLA Ops:
  7.2 0.9 multiply_convert_fusion
  8.4 0.9 reshape.65
  9.3 1.2 select_reduce_fusion.5
  10.5 1.4 select_reduce_fusion.4
  12.8 0.5 fusion.26
  13.3 23.1 %all-reduce = (f32[32]{0:T(128)S(1)}, f32[32]{0:T(128)S(1)}) all-reduce(f32[32]{0:T(128)S(1)} %get-tuple-element.192, f32[32]{0:T(128)S(1)} %get-tuple-element.191), channel_id=1, replica_groups=mesh['rows'=8,'feat'=4] {'rows'}, use_global_device_ids=true, to_apply=%region_12.13 | all-reduce | flops 64 | bytes 512 | tf_op jit(solution)/shard_map/psum | solution.py:110
  36.9 0.6 fusion.31
  37.6 22.8 %while.23 = (s32[]{:T(128)}, f32[4,16,256]{2,1,0:T(8,128)S(1)}, s32[15,4,1024]{2,1,0:T(4,128)S(1)}, s32[15,1024]{1,0:T(8,128)S(1)}, bf16[15,1024]{1,0:T(8,128)(2...) while((s32[]{:T(128)}, f32[4,16,256]{2,1,0:T(8,128)S(1)}, ...), condition=%wide.region_7.8_spmd.clone, body=%wide.region_6.7_spmd.clone.sunk | while | flops 34725888 | bytes 270443 | solution.py:56
  37.7 1.4 fusion.39
  39.3 1.4 fusion.39
  40.8 1.4 fusion.39
  42.3 1.4 fusion.39
  43.8 1.4 fusion.39
  45.4 1.4 fusion.39
  46.9 1.4 fusion.39
  48.4 1.4 fusion.39
  49.9 1.4 fusion.39
  51.4 1.4 fusion.39
  53.0 1.4 fusion.39
  54.5 1.4 fusion.39
  56.0 1.4 fusion.39
  57.5 1.4 fusion.39
  59.0 1.4 fusion.39
  60.5 0.6 copy-done.6
  61.1 22.8 %while.22 = (s32[]{:T(128)}, f32[4,16,256]{2,1,0:T(8,128)S(1)}, s32[15,4,1024]{2,1,0:T(4,128)S(1)}, s32[15,1024]{1,0:T(8,128)S(1)}, bf16[15,1024]{1,0:T(8,128)(2...) while((s32[]{:T(128)}, f32[4,16,256]{2,1,0:T(8,128)S(1)}, ...), condition=%wide.region_1.2_spmd.clone, body=%wide.region_0.1_spmd.clone.sunk | while | flops 34725888 | bytes 270443 | solution.py:56
  61.2 1.4 fusion.37
  62.7 1.4 fusion.37
  64.2 1.4 fusion.37
  65.8 1.4 fusion.37
  67.3 1.4 fusion.37
  68.8 1.4 fusion.37
  70.3 1.4 fusion.37
  71.8 1.4 fusion.37
  73.4 1.4 fusion.37
  74.9 1.4 fusion.37
  76.4 1.4 fusion.37
  77.9 1.4 fusion.37
  79.4 1.4 fusion.37
  81.0 1.4 fusion.37
  82.5 1.4 fusion.37
  83.9 0.6 copy-done.5
  84.6 17.7 %psum.39 = f32[]{:T(128)} all-reduce(f32[]{:T(128)} %fusion.31), channel_id=1, replica_groups=mesh['rows'=8,'feat'=4] {'rows'}, use_global_device_ids=true, to_apply=%region_16.17 | all-reduce | flops 1 | bytes 8 | tf_op jit(solution)/shard_map/psum | solution.py:116
  102.9 0.7 broadcast_multiply_fusion
  103.6 48.3 %all-reduce.4.cloned.1.call-done = (f32[4,16,256]{2,1,0:T(8,128)}, f32[4,16,256]{2,1,0:T(8,128)}) async-done(((f32[4,16,256]{2,1,0:T(8,128)}, f32[4,16,256]{2,1,0:T(8,128)}), (f32[4,16,256]{2,1,0:T(8,128)}, f32[4,16,256]{2,1,0:T(8,128)})) %all-reduce.4.cloned.1.call-update) | async-done | bytes 131088 | tf_op jit(solution)/shard_map/psum | solution.py:63
  151.9 0.8 slice_bitcast_fusion.3
  152.7 0.9 sub.3
  153.8 0.7 pad_maximum_fusion
  154.5 0.6 copy.34
  (164 shorter events, 4.4 us)
Async XLA Ops:
  7.2 4.8 %copy-start.1 = (s32[15360]{0:T(1024)S(1)}, s32[15360]{0:T(1024)}, u32[]{:S(2)}) copy-start(s32[15360]{0:T(1024)} %param.14) | copy-start | bytes 184324
  7.2 144.7 %all-reduce.4.cloned.1.call-start = ((), (), s32[]{:S(2)}) async-start(), calls=%async_computation | async-start | bytes 262144 | tf_op jit(solution)/shard_map/psum | solution.py:63
  8.1 3.9 %copy-start.8 = (s32[16]{0:T(128)S(1)}, s32[16]{0:T(128)}, u32[]{:S(2)}) copy-start(s32[16]{0:T(128)} %param.21) | copy-start | bytes 196
  8.2 3.9 %copy-start.9 = (s32[16]{0:T(128)S(1)}, s32[16]{0:T(128)}, u32[]{:S(2)}) copy-start(s32[16]{0:T(128)} %param.20) | copy-start | bytes 196
  8.3 4.2 %copy-start = (s32[16,15360]{1,0:T(8,128)S(1)}, s32[16,15360]{1,0:T(8,128)}, u32[]{:S(2)}) copy-start(s32[16,15360]{1,0:T(8,128)} %param.13) | copy-start | bytes 2949124
  12.8 24.1 %copy-start.2 = (f32[15360]{0:T(1024)S(1)}, f32[15360]{0:T(1024)}, u32[]{:S(2)}) copy-start(f32[15360]{0:T(1024)} %param.16) | copy-start | bytes 184324
  12.8 24.1 %copy-start.3 = (f32[15360]{0:T(1024)S(1)}, f32[15360]{0:T(1024)}, u32[]{:S(2)}) copy-start(f32[15360]{0:T(1024)} %param.15) | copy-start | bytes 184324
  36.5 1.2 copy-start.10
  60.4 0.6 copy-start.6
  60.5 42.4 %copy-start.7 = (f32[15360]{0:T(1024)S(1)}, f32[15360]{0:T(1024)}, u32[]{:S(2)}) copy-start(f32[15360]{0:T(1024)} %param.17) | copy-start | bytes 184324
  83.9 0.6 copy-start.5
  151.9 2.6 %copy-start.4 = (f32[4,16,256]{2,1,0:T(8,128)S(1)}, f32[4,16,256]{2,1,0:T(8,128)}, u32[]{:S(2)}) copy-start(f32[4,16,256]{2,1,0:T(8,128)} %get-tuple-element.333) | copy-start | bytes 196612
Sparse Core Ops, SparseCore 0:
  84.7 67.1 all-reduce.3
where the time goes:
time: 162 us
  waiting for transfers between devices  48.3 us (30%)
  matrix products  42.6 us (26%)
  blocking collectives  40.8 us (25%)
  between operations  15 us (9%)
  other arithmetic  7.97 us (5%)
  local copies, waits for them, and re-layouts  6.41 us (4%)
    psum x1, waiting for transfers between devices, combine_rows(): return lax.psum(partial_value, 'rows')  48.3 us
    dot_general x30, matrix products, accumulate(): jnp.einsum('rn,frb->fnb', row_matrix, onehot_bins, preferred_element_type...  42.1 us
    psum x1, blocking collectives, on_device(): leaf_weight, leaf_signed = lax.psum((local_sums[0], local_sums[1]), 'rows')  23.1 us
    psum x1, blocking collectives, on_device(): grand_sum = lax.psum(jnp.sum(raw_weights), 'rows')  17.7 us
  transfers between devices with their start and end apart: 1, of which 1 were waited for; matrix products, arithmetic and copies ran while one was open for 0% of the time, Pallas kernels for 0%

commit v1 on v0

v1 whole, which is shorter than its diff:
```python
import functools

import jax
import jax.numpy as jnp
from jax import lax
from jax.experimental import pallas as pl
from jax.experimental.pallas import tpu as pltpu
from jax.sharding import PartitionSpec as P

BINS = 256
LANES = 128
SUB = 8
NT = (((1,), (1,)), ((), ()))


def grow_kernel(
    own_ref,
    f3_ref,
    b3_ref,
    f4_ref,
    b4_ref,
    codes_ref,
    node_ref,
    label_ref,
    weight_ref,
    hist_ref,
    path_ref,
    low_ref,
    slot_ref,
    high_ref,
    mid_ref,
    rest_ref,
):
    groups = node_ref.shape[0]
    steps = groups // SUB
    own = low_ref.shape[0]
    nodes3 = f3_ref.shape[0]
    nodes4 = f4_ref.shape[0]
    tag_count = 2 * nodes4
    paths = 4 * nodes4

    def code_block(feature, step):
        start = (feature // SUB) * (groups * SUB) + step * (SUB * SUB) + feature % SUB
        return codes_ref[pl.ds(start, SUB, stride=SUB), :]

    def route(step, carry):
        rows = pl.ds(step * SUB, SUB)
        node = node_ref[rows, :]
        positive = jnp.where(label_ref[rows, :] > 0, 1, 0)
        weight = weight_ref[rows, :]
        right3 = jnp.zeros((SUB, LANES), jnp.int32)
        for n in range(nodes3):
            above = jnp.where(code_block(f3_ref[n], step) > b3_ref[n], 1, 0)
            right3 = jnp.where(node == n, above, right3)
        node4 = 2 * node + right3
        right4 = jnp.zeros((SUB, LANES), jnp.int32)
        for n in range(nodes4):
            above = jnp.where(code_block(f4_ref[n], step) > b4_ref[n], 1, 0)
            right4 = jnp.where(node4 == n, above, right4)
        tag = right3 * (2 * nodes3) + positive * nodes3 + node
        path_ref[rows, :] = positive * (2 * nodes4) + 2 * node4 + right4
        for i in range(own):
            code = code_block(own_ref[0] + i, step)
            low_ref[i, rows, :] = code & (LANES - 1)
            slot_ref[i, rows, :] = (code // LANES) * tag_count + tag
        high = weight.astype(jnp.bfloat16).astype(jnp.float32)
        mid = (weight - high).astype(jnp.bfloat16).astype(jnp.float32)
        high_ref[rows, :] = high
        mid_ref[rows, :] = mid
        rest_ref[rows, :] = weight - high - mid
        return carry

    lax.fori_loop(0, steps, route, 0)
    hist_ref[...] = jnp.zeros_like(hist_ref)
    cell = (2 * SUB, LANES)
    iota = lax.broadcasted_iota(jnp.int32, cell, 0)
    small = jnp.int16
    ranks = [(iota + 2 * SUB * g).astype(small) for g in range(LANES // (2 * SUB))]
    one = jnp.ones(cell, jnp.bfloat16)
    nothing = jnp.zeros(cell, jnp.bfloat16)

    def spread(ref, row, dtype, *lead):
        line = ref[(*lead, pl.ds(row, 1), slice(None))]
        return jnp.broadcast_to(line, cell).astype(dtype)

    def onehot(value, count, filled):
        parts = [jnp.where(value == ranks[g], filled, nothing) for g in range(count // (2 * SUB))]
        return jnp.concatenate(parts, axis=0)

    def tally(step, carry):
        base = step * SUB
        lines = range(SUB)
        heavy = [spread(high_ref, base + k, jnp.bfloat16) for k in lines]
        for i in range(own):
            slots = jnp.concatenate(
                [
                    onehot(spread(slot_ref, base + k, small, i), 2 * tag_count, heavy[k])
                    for k in lines
                ],
                axis=1,
            )
            lows = jnp.concatenate(
                [onehot(spread(low_ref, base + k, small, i), LANES, one) for k in lines],
                axis=1,
            )
            part = pl.ds(i * 2 * tag_count, 2 * tag_count)
            hist_ref[part, :] += lax.dot_general(
                slots, lows, NT, preferred_element_type=jnp.float32
            )
        pieces = []
        for k in lines:
            mid = spread(mid_ref, base + k, jnp.bfloat16)
            rest = spread(rest_ref, base + k, jnp.bfloat16)
            pieces.append(
                jnp.where(
                    ranks[0] == 0,
                    heavy[k],
                    jnp.where(ranks[0] == 1, mid, jnp.where(ranks[0] == 2, rest, nothing)),
                )
            )
        trails = jnp.concatenate(
            [onehot(spread(path_ref, base + k, small), LANES, one) for k in lines], axis=1
        )
        part = pl.ds(own * 2 * tag_count, 2 * SUB)
        hist_ref[part, :] += lax.dot_general(
            jnp.concatenate(pieces, axis=1), trails, NT, preferred_element_type=jnp.float32
        )
        return carry

    lax.fori_loop(0, steps, tally, 0)


def finish_kernel(
    total,
    hist_ref,
    path_ref,
    label_ref,
    weight_ref,
    score_ref,
    hist3_ref,
    hist4_ref,
    value_ref,
    new_score_ref,
    new_weight_ref,
    weave_ref,
):
    own, rows4, _ = hist4_ref.shape
    tags = rows4
    nodes4 = tags // 2
    nodes3 = nodes4 // 2
    leaves = value_ref.shape[1]
    for i in range(own):
        base = i * 2 * tags
        for h in range(2):
            lanes = slice(h * LANES, (h + 1) * LANES)
            start = base + h * tags

            def tag_rows(right, positive):
                first = start + right * 2 * nodes3 + positive * nodes3
                return hist_ref[first : first + nodes3, :]

            sums = [tag_rows(r, 1) + tag_rows(r, 0) for r in range(2)]
            diffs = [tag_rows(r, 1) - tag_rows(r, 0) for r in range(2)]
            hist3_ref[i, 0:nodes3, lanes] = sums[0] + sums[1]
            hist3_ref[i, nodes3 : 2 * nodes3, lanes] = diffs[0] + diffs[1]
            for r in range(2):
                weave_ref[pl.ds(start + r, nodes3, stride=2), :] = sums[r]
                weave_ref[pl.ds(start + nodes4 + r, nodes3, stride=2), :] = diffs[r]
            hist4_ref[i, :, lanes] = weave_ref[start : start + tags, :]
    leaf_base = own * 2 * tags
    pieces = hist_ref[leaf_base : leaf_base + SUB, :]
    lane = lax.broadcasted_iota(jnp.int32, (1, LANES), 1)
    rounded = pieces[0:1, :]
    full = pieces[0:1, :] + (pieces[1:2, :] + pieces[2:3, :])
    other = pltpu.roll(rounded, LANES - leaves, 1)
    values = (other - rounded) / (other + rounded + 1.0)
    value_ref[...] = values[:, 0:leaves]
    negative = lane < leaves
    both = jnp.where(negative, values, pltpu.roll(values, leaves, 1))
    both = jnp.where(lane < 2 * leaves, both, 0.0)
    growth = jnp.exp(jnp.where(negative, both, -both))
    grand = jnp.sum(full * growth, axis=1, keepdims=True)
    factor = growth * (total / grand)
    factor8 = jnp.broadcast_to(factor, (SUB, LANES))
    both8 = jnp.broadcast_to(both, (SUB, LANES))
    for step in range(path_ref.shape[0] // SUB):
        rows = slice(step * SUB, (step + 1) * SUB)
        path = path_ref[rows, :]
        scale = jnp.take_along_axis(factor8, path, axis=1)
        shift = jnp.take_along_axis(both8, path, axis=1)
        new_weight_ref[rows, :] = weight_ref[rows, :] * scale
        new_score_ref[rows, :] = score_ref[rows, :] + shift


def combine_rows(part, axis, size):
    if size & (size - 1):
        return lax.psum(part, axis)
    reach = 1
    while reach < size:
        pairs = [(i, i ^ reach) for i in range(size)]
        part = part + lax.ppermute(part, axis, pairs)
        reach *= 2
    return part


def whole(memory=pltpu.VMEM):
    return pl.BlockSpec(memory_space=memory)


def on_device(
    row_parts,
    feat_parts,
    bin_codes,
    node_ids,
    labels,
    weights,
    predictions,
    level3_feature,
    level3_bin,
    level4_feature,
    level4_bin,
):
    features, row_count = bin_codes.shape
    groups = row_count // LANES
    own = features // feat_parts
    nodes3 = level3_feature.shape[0]
    nodes4 = level4_feature.shape[0]
    leaves = 2 * nodes4
    tags = 2 * nodes4
    first = (lax.axis_index("feat") * own).astype(jnp.int32).reshape(1)
    codes = (
        bin_codes.reshape(features // SUB, SUB, groups, LANES)
        .transpose(0, 2, 1, 3)
        .reshape(features * groups, LANES)
    )
    square = (groups, LANES)
    node_sq = node_ids.reshape(square)
    label_sq = labels.reshape(square)
    weight_sq = weights.reshape(square)
    score_sq = predictions.reshape(square)
    hist_rows = own * 2 * tags + 2 * SUB
    f32 = jnp.float32
    hist, path = pl.pallas_call(
        grow_kernel,
        out_shape=(
            jax.ShapeDtypeStruct((hist_rows, LANES), f32),
            jax.ShapeDtypeStruct(square, jnp.int32),
        ),
        in_specs=[whole(pltpu.SMEM)] * 5 + [whole()] * 4,
        out_specs=(whole(), whole()),
        scratch_shapes=[
            pltpu.VMEM((own, *square), jnp.int32),
            pltpu.VMEM((own, *square), jnp.int32),
            pltpu.VMEM(square, f32),
            pltpu.VMEM(square, f32),
            pltpu.VMEM(square, f32),
        ],
        compiler_params=pltpu.CompilerParams(vmem_limit_bytes=24 * 1024 * 1024),
    )(first, level3_feature, level3_bin, level4_feature, level4_bin, codes, node_sq, label_sq, weight_sq)
    hist = combine_rows(hist, "rows", row_parts)
    hist3, hist4, values, new_scores, new_weights = pl.pallas_call(
        functools.partial(finish_kernel, float(row_count * row_parts)),
        out_shape=(
            jax.ShapeDtypeStruct((own, 2 * nodes3, BINS), f32),
            jax.ShapeDtypeStruct((own, 2 * nodes4, BINS), f32),
            jax.ShapeDtypeStruct((1, leaves), f32),
            jax.ShapeDtypeStruct(square, f32),
            jax.ShapeDtypeStruct(square, f32),
        ),
        in_specs=[whole()] * 5,
        out_specs=(whole(),) * 5,
        scratch_shapes=[pltpu.VMEM((own * 2 * tags, LANES), f32)],
        compiler_params=pltpu.CompilerParams(vmem_limit_bytes=24 * 1024 * 1024),
    )(hist, path, label_sq, weight_sq, score_sq)
    return (
        hist3,
        hist4,
        values.reshape(leaves),
        new_scores.reshape(row_count),
        new_weights.reshape(row_count),
    )


def solution(mesh):
    placed = (P(None, "rows"), P("rows"), P("rows"), P("rows"), P("rows"), P(), P(), P(), P())
    return jax.shard_map(
        functools.partial(on_device, mesh.shape["rows"], mesh.shape["feat"]),
        mesh=mesh,
        in_specs=placed,
        out_specs=(P("feat", None, None), P("feat", None, None), P(), P("rows"), P("rows")),
        check_vma=False,
    )
```

time: 162 us -> 37.9 us (0.23)
  matrix products: 42.6 us -> 0 us
  blocking collectives: 40.8 us -> 0 us
  waiting for transfers between devices: 48.3 us -> 11.7 us
  between operations: 15 us -> 0.7 us
  Pallas kernels: 0 us -> 13 us
  other arithmetic: 7.97 us -> 0.06 us
  starting transfers between devices: 0.04 us -> 7.73 us
  local copies, waits for them, and re-layouts: 6.41 us -> 4.36 us
    psum x1 -> x0, waiting for transfers between devices: 48.3 us -> none  [combine_rows(): return lax.psum(partial_value, 'rows')]
    dot_general x31 -> x0, matrix products: 42.6 us -> none  [the longest x30 42.1 us: accumulate(): jnp.einsum('rn,frb->fnb', row_matrix, onehot_bins, preferred_element_type...]
    psum x2 -> x0, blocking collectives: 40.8 us -> none  [the longest x1 23.1 us: on_device(): leaf_weight, leaf_signed = lax.psum((local_sums[0], local_sums[1]), 'rows')]
    pallas_call x0 -> x2, Pallas kernels: none -> 13 us  [the longest x1 12 us: on_device(): pl.pallas_call(grow_kernel, out_shape=(jax.ShapeDtypeStruct((hist_rows, L...]
    ppermute x0 -> x3, waiting for transfers between devices: none -> 11.7 us  [combine_rows(): part = part + lax.ppermute(part, axis, pairs)]
    ppermute x0 -> x3, starting transfers between devices: none -> 7.73 us  [combine_rows(): part = part + lax.ppermute(part, axis, pairs)]
    reduce_sum x6 -> x0, other arithmetic: 4.41 us -> none  [the longest x2 1.71 us: routing(): picked = jnp.sum(jnp.where(owner_mask, bin_codes, 0), axis=0)]
    unnamed x23 -> x18, local copies, waits for them, and re-layouts: 1.95 us -> 4.36 us
  transfers between devices with their start and end apart: 1 -> 3, of which waited for: 1 -> 3; matrix products, arithmetic and copies ran while one was open for 0% -> 0% of each run, Pallas kernels for 0% -> 0%
where the time goes in v1:
time: 37.9 us; the launch traced here: 37.6 us
  Pallas kernels  13 us (34%)
  waiting for transfers between devices  11.7 us (31%)
  starting transfers between devices  7.73 us (20%)
  local copies, waits for them, and re-layouts  4.36 us (12%)
  between operations  0.7 us (2%)
    pallas_call x1, Pallas kernels, on_device(): pl.pallas_call(grow_kernel, out_shape=(jax.ShapeDtypeStruct((hist_rows, L...  12 us
    ppermute x3, waiting for transfers between devices, combine_rows(): part = part + lax.ppermute(part, axis, pairs)  11.7 us
    ppermute x3, starting transfers between devices, combine_rows(): part = part + lax.ppermute(part, axis, pairs)  7.73 us
    unnamed x18, local copies, waits for them, and re-layouts  4.36 us
    pallas_call x1, Pallas kernels, on_device(): pl.pallas_call(functools.partial(finish_kernel, float(row_count * row_par...  1.02 us
  transfers between devices with their start and end apart: 3, of which 3 were waited for; matrix products, arithmetic and copies ran while one was open for 0% of the time, Pallas kernels for 0%

profile of v1, /device:TPU:0, one launch (start us, length us, event | category | flops | bytes accessed | tf_op | source)
XLA Modules:
  0.0 37.6 jit_solution(5703539369018817478)
XLA Ops:
  0.6 0.0 copy-start.8
  0.6 0.0 copy-start.5
  0.7 0.0 copy-start.6
  0.7 0.0 copy-start.7
  0.7 0.6 %copy-done.8 = s32[16]{0:T(128)S(1)} copy-done((s32[16]{0:T(128)S(1)}, s32[16]{0:T(128)}, u32[]{:S(2)}) %copy-start.8) | copy-done | bytes 88
  1.3 0.0 copy-done.5
  1.3 0.0 copy-done.6
  1.3 0.0 copy-done.7
  1.3 0.0 copy-start
  1.3 1.2 %copy-done = s32[16,15360]{1,0:T(8,128)S(1)} copy-done((s32[16,15360]{1,0:T(8,128)S(1)}, s32[16,15360]{1,0:T(8,128)}, u32[]{:S(2)}) %copy-start) | copy-done | bytes 983064
  2.5 0.0 copy-start.1
  2.5 0.8 %copy-done.1 = f32[15360]{0:T(1024)S(1)} copy-done((f32[15360]{0:T(1024)S(1)}, f32[15360]{0:T(1024)}, u32[]{:S(2)}) %copy-start.1) | copy-done | bytes 61464
  3.4 0.0 copy-start.2
  3.4 0.8 %copy-done.2 = f32[15360]{0:T(1024)S(1)} copy-done((f32[15360]{0:T(1024)S(1)}, f32[15360]{0:T(1024)}, u32[]{:S(2)}) %copy-start.2) | copy-done | bytes 61464
  4.2 0.0 copy-start.3
  4.2 0.8 %copy-done.3 = s32[15360]{0:T(1024)S(1)} copy-done((s32[15360]{0:T(1024)S(1)}, s32[15360]{0:T(1024)}, u32[]{:S(2)}) %copy-start.3) | copy-done | bytes 61464
  5.0 12.0 %shard_map.128 = (f32[272,128]{1,0:T(8,128)S(1)}, s32[120,128]{1,0:T(8,128)S(1)}) custom-call(s32[1]{0:T(128)} %bitcast.own_ref, s32[8]{0:T(128)S(1)} %copy-done.5, s32[8]{0:T(128)S(1)} %copy-done.6, s32[16]{0:T(128)S(1)} %copy-done.7, s32[16]{0:T(128)S(1)} %copy-done.8, s32[1920,128]{1,0:T(8,128)S(1)} %bitcast.13, s32[120,128]{1,0:T(8,128)S(1)} %bitcast.18, ...), custom_call_target="tpu_custom_call" | custom-call | tf_op jit(solution)/shard_map/pallas_call | solution.py:243
  17.0 3.0 %collective-permute-start = (f32[272,128]{1,0:T(8,128)S(1)}, f32[272,128]{1,0:T(8,128)S(1)}, u32[]{:S(2)}, u32[]{:S(2)}) collective-permute-start(f32[272,128]{1,0:T(8,128)S(1)} %get-tuple-element.12), channel_id=1, source_target_pairs={{0,4},{4,0},{8,12},{12,8},{16,20},{20,16},{24,28},{28,24},{1,5},{5... | collective-permute-start | bytes 417800 | tf_op jit(solution)/shard_map/ppermute | solution.py:201
  20.0 3.7 %collective-permute-done = f32[272,128]{1,0:T(8,128)S(1)} collective-permute-done((f32[272,128]{1,0:T(8,128)S(1)}, f32[272,128]{1,0:T(8,128)S(1)}, u32[]{:S(2)}, u32[]{:S(2)}) %collective-permute-start) | collective-permute-done | bytes 139296 | tf_op jit(solution)/shard_map/ppermute | solution.py:201
  23.7 1.9 %collective-permute-start.1 = (f32[272,128]{1,0:T(8,128)S(1)}, f32[272,128]{1,0:T(8,128)S(1)}, u32[]{:S(2)}, u32[]{:S(2)}) collective-permute-start(f32[272,128]{1,0:T(8,128)S(1)} %add.9), channel_id=1, source_target_pairs={{0,8},{4,12},{8,0},{12,4},{16,24},{20,28},{24,16},{28,20},{1,9},{5... | collective-permute-start | bytes 417800 | tf_op jit(solution)/shard_map/ppermute | solution.py:201
  25.6 3.3 %collective-permute-done.1 = f32[272,128]{1,0:T(8,128)S(1)} collective-permute-done((f32[272,128]{1,0:T(8,128)S(1)}, f32[272,128]{1,0:T(8,128)S(1)}, u32[]{:S(2)}, u32[]{:S(2)}) %collective-permute-start.1) | collective-permute-done | bytes 139296 | tf_op jit(solution)/shard_map/ppermute | solution.py:201
  28.9 0.0 copy-start.4
  28.9 2.9 %collective-permute-start.2 = (f32[272,128]{1,0:T(8,128)S(1)}, f32[272,128]{1,0:T(8,128)S(1)}, u32[]{:S(2)}, u32[]{:S(2)}) collective-permute-start(f32[272,128]{1,0:T(8,128)S(1)} %add.10), channel_id=1, source_target_pairs={{0,16},{4,20},{8,24},{12,28},{16,0},{20,4},{24,8},{28,12},{1,17},{... | collective-permute-start | bytes 417800 | tf_op jit(solution)/shard_map/ppermute | solution.py:201
  31.8 4.8 %collective-permute-done.2 = f32[272,128]{1,0:T(8,128)S(1)} collective-permute-done((f32[272,128]{1,0:T(8,128)S(1)}, f32[272,128]{1,0:T(8,128)S(1)}, u32[]{:S(2)}, u32[]{:S(2)}) %collective-permute-start.2) | collective-permute-done | bytes 139296 | tf_op jit(solution)/shard_map/ppermute | solution.py:201
  36.6 0.0 copy-done.4
  36.6 1.0 %shard_map.129 = (f32[4,16,256]{2,1,0:T(8,128)}, f32[4,32,256]{2,1,0:T(8,128)}, f32[1,32]{1,0:T(1,128)}, f32[120,128]{1,0:T(8,128)}, f32[120,128]{1,0:T(8,128)}) custom-call(f32[272,128]{1,0:T(8,128)S(1)} %add.11.hist_ref, s32[120,128]{1,0:T(8,128)S(1)} %get-tuple-element.13.path_ref, f32[120,128]{1,0:T(8,128)S(1)} %bitcast.15, f32[120,128]{1,0:T(8,128)S(1)} %bitcast.17, ...), custom_call_target="tpu_custom_call" | custom-call | tf_op jit(solution)/shard_map/pallas_call | solution.py:261
  (3 shorter events, 0.1 us)
Async XLA Ops:
  0.6 0.7 %copy-start.8 = (s32[16]{0:T(128)S(1)}, s32[16]{0:T(128)}, u32[]{:S(2)}) copy-start(s32[16]{0:T(128)} %b4_ref.1) | copy-start | bytes 196
  0.6 0.7 %copy-start.5 = (s32[8]{0:T(128)S(1)}, s32[8]{0:T(128)}, u32[]{:S(2)}) copy-start(s32[8]{0:T(128)} %f3_ref.1) | copy-start | bytes 100
  0.7 0.7 %copy-start.6 = (s32[8]{0:T(128)S(1)}, s32[8]{0:T(128)}, u32[]{:S(2)}) copy-start(s32[8]{0:T(128)} %b3_ref.1) | copy-start | bytes 100
  0.7 0.7 %copy-start.7 = (s32[16]{0:T(128)S(1)}, s32[16]{0:T(128)}, u32[]{:S(2)}) copy-start(s32[16]{0:T(128)} %f4_ref.1) | copy-start | bytes 196
  1.3 1.2 %copy-start = (s32[16,15360]{1,0:T(8,128)S(1)}, s32[16,15360]{1,0:T(8,128)}, u32[]{:S(2)}) copy-start(s32[16,15360]{1,0:T(8,128)} %param.9) | copy-start | bytes 2949124
  2.5 0.8 %copy-start.1 = (f32[15360]{0:T(1024)S(1)}, f32[15360]{0:T(1024)}, u32[]{:S(2)}) copy-start(f32[15360]{0:T(1024)} %param.11) | copy-start | bytes 184324
  3.4 0.8 %copy-start.2 = (f32[15360]{0:T(1024)S(1)}, f32[15360]{0:T(1024)}, u32[]{:S(2)}) copy-start(f32[15360]{0:T(1024)} %param.12) | copy-start | bytes 184324
  4.2 0.8 %copy-start.3 = (s32[15360]{0:T(1024)S(1)}, s32[15360]{0:T(1024)}, u32[]{:S(2)}) copy-start(s32[15360]{0:T(1024)} %param.10) | copy-start | bytes 184324
  17.0 6.7 %collective-permute-start = (f32[272,128]{1,0:T(8,128)S(1)}, f32[272,128]{1,0:T(8,128)S(1)}, u32[]{:S(2)}, u32[]{:S(2)}) collective-permute-start(f32[272,128]{1,0:T(8,128)S(1)} %get-tuple-element.12), channel_id=1, source_target_pairs={{0,4},{4,0},{8,12},{12,8},{16,20},{20,16},{24,28},{28,24},{1,5},{5... | collective-permute-start | bytes 417800 | tf_op jit(solution)/shard_map/ppermute | solution.py:201
  23.7 5.1 %collective-permute-start.1 = (f32[272,128]{1,0:T(8,128)S(1)}, f32[272,128]{1,0:T(8,128)S(1)}, u32[]{:S(2)}, u32[]{:S(2)}) collective-permute-start(f32[272,128]{1,0:T(8,128)S(1)} %add.9), channel_id=1, source_target_pairs={{0,8},{4,12},{8,0},{12,4},{16,24},{20,28},{24,16},{28,20},{1,9},{5... | collective-permute-start | bytes 417800 | tf_op jit(solution)/shard_map/ppermute | solution.py:201
  28.9 7.7 %copy-start.4 = (f32[15360]{0:T(1024)S(1)}, f32[15360]{0:T(1024)}, u32[]{:S(2)}) copy-start(f32[15360]{0:T(1024)} %param.13) | copy-start | bytes 184324
  28.9 7.7 %collective-permute-start.2 = (f32[272,128]{1,0:T(8,128)S(1)}, f32[272,128]{1,0:T(8,128)S(1)}, u32[]{:S(2)}, u32[]{:S(2)}) collective-permute-start(f32[272,128]{1,0:T(8,128)S(1)} %add.10), channel_id=1, source_target_pairs={{0,16},{4,20},{8,24},{12,28},{16,0},{20,4},{24,8},{28,12},{1,17},{... | collective-permute-start | bytes 417800 | tf_op jit(solution)/shard_map/ppermute | solution.py:201

commit v2 on v1

v2 whole, which is shorter than its diff:
```python
import functools

import jax
import jax.numpy as jnp
from jax import lax
from jax.experimental import pallas as pl
from jax.experimental.pallas import tpu as pltpu
from jax.sharding import PartitionSpec as P

BINS = 256
LANES = 128
SUB = 8
NT = (((1,), (1,)), ((), ()))


def grow_kernel(
    f3_hbm,
    b3_hbm,
    f4_hbm,
    b4_hbm,
    codes_hbm,
    node_hbm,
    label_hbm,
    weight_hbm,
    hist_ref,
    path_ref,
    f3_ref,
    b3_ref,
    f4_ref,
    b4_ref,
    codes_ref,
    node_ref,
    label_ref,
    weight_ref,
    low_ref,
    slot_ref,
    high_ref,
    sums_ref,
    leaf_ref,
    sems,
):
    groups = node_ref.shape[0]
    steps = groups // SUB
    own = low_ref.shape[0]
    nodes3 = f3_ref.shape[0]
    nodes4 = f4_ref.shape[0]
    tag_count = 2 * nodes4
    paths = 4 * nodes4
    moves = [
        pltpu.make_async_copy(source, target, sems.at[i])
        for i, (source, target) in enumerate(
            (
                (codes_hbm, codes_ref),
                (node_hbm, node_ref),
                (f3_hbm, f3_ref),
                (b3_hbm, b3_ref),
                (f4_hbm, f4_ref),
                (b4_hbm, b4_ref),
                (label_hbm, label_ref),
                (weight_hbm, weight_ref),
            )
        )
    ]
    for move in moves:
        move.start()
    sums_ref[...] = jnp.zeros_like(sums_ref)
    leaf_ref[...] = jnp.zeros_like(leaf_ref)
    for move in moves:
        move.wait()

    def code_start(feature):
        return (feature // SUB) * (groups * SUB) + feature % SUB

    def code_block(start, step):
        return codes_ref[pl.ds(start + step * (SUB * SUB), SUB, stride=SUB), :]

    def goes_right(nodes, feature_ref, bin_ref):
        margin = [jnp.zeros((SUB, LANES), jnp.int32) for _ in nodes]
        for n in range(feature_ref.shape[0]):
            start = code_start(feature_ref[n])
            cut = bin_ref[n]
            for step, node in enumerate(nodes):
                margin[step] = jnp.where(node == n, code_block(start, step) - cut, margin[step])
        return [jnp.where(m > 0, 1, 0) for m in margin]

    def rows_of(step):
        return slice(step * SUB, (step + 1) * SUB)

    node3 = [node_ref[rows_of(step), :] for step in range(steps)]
    right3 = goes_right(node3, f3_ref, b3_ref)
    node4 = [2 * n + r for n, r in zip(node3, right3)]
    right4 = goes_right(node4, f4_ref, b4_ref)
    first = lax.axis_index("feat") * own
    starts = [code_start(first + i) for i in range(own)]
    for step in range(steps):
        rows = rows_of(step)
        positive = jnp.where(label_ref[rows, :] > 0, 1, 0)
        tag = right3[step] * (2 * nodes3) + positive * nodes3 + node3[step]
        path_ref[rows, :] = positive * (2 * nodes4) + 2 * node4[step] + right4[step]
        for i in range(own):
            code = code_block(starts[i], step)
            low_ref[i, rows, :] = code & (LANES - 1)
            slot_ref[i, rows, :] = (code // LANES) * tag_count + tag
        high_ref[rows, :] = weight_ref[rows, :].astype(jnp.bfloat16).astype(jnp.float32)

    cell = (2 * SUB, LANES)
    iota = lax.broadcasted_iota(jnp.int32, cell, 0)
    small = jnp.int16
    ranks = [(iota + 2 * SUB * g).astype(small) for g in range(LANES // (2 * SUB))]
    one = jnp.ones(cell, jnp.bfloat16)
    nothing = jnp.zeros(cell, jnp.bfloat16)
    leaf_rank = [
        lax.broadcasted_iota(jnp.int32, (SUB, LANES), 0) + SUB * g for g in range(paths // SUB)
    ]

    def spread(ref, row, dtype, *lead):
        line = ref[(*lead, pl.ds(row, 1), slice(None))]
        return jnp.broadcast_to(line, cell).astype(dtype)

    def wide(ref, row):
        return jnp.broadcast_to(ref[pl.ds(row, 1), :], (SUB, LANES))

    def onehot(value, count, filled):
        parts = [jnp.where(value == ranks[g], filled, nothing) for g in range(count // (2 * SUB))]
        return jnp.concatenate(parts, axis=0)

    span = next(n for n in (24, 16, 8) if groups % n == 0)

    def tally(turn, carry):
        base = turn * span
        lines = range(span)
        heavy = [spread(high_ref, base + k, jnp.bfloat16) for k in lines]
        for i in range(own):
            slots = jnp.concatenate(
                [
                    onehot(spread(slot_ref, base + k, small, i), 2 * tag_count, heavy[k])
                    for k in lines
                ],
                axis=1,
            )
            lows = jnp.concatenate(
                [onehot(spread(low_ref, base + k, small, i), LANES, one) for k in lines],
                axis=1,
            )
            sums_ref[i] += lax.dot_general(lows, slots, NT, preferred_element_type=jnp.float32)
        count = paths // SUB
        exact = [leaf_ref[0, rows_of(g), :] for g in range(count)]
        rounded = [leaf_ref[1, rows_of(g), :] for g in range(count)]
        for k in lines:
            path = wide(path_ref, base + k)
            weight = wide(weight_ref, base + k)
            high = wide(high_ref, base + k)
            for g in range(count):
                here = path == leaf_rank[g]
                exact[g] += jnp.where(here, weight, 0.0)
                rounded[g] += jnp.where(here, high, 0.0)
        for g in range(count):
            leaf_ref[0, rows_of(g), :] = exact[g]
            leaf_ref[1, rows_of(g), :] = rounded[g]
        return carry

    lax.fori_loop(0, groups // span, tally, 0)
    for i in range(own // 2):
        hist_ref[i * LANES : (i + 1) * LANES, :] = jnp.concatenate(
            [sums_ref[2 * i], sums_ref[2 * i + 1]], axis=1
        )
    spot = lax.broadcasted_iota(jnp.int32, (paths, LANES), 0)
    lane = lax.broadcasted_iota(jnp.int32, (paths, LANES), 1)
    lines = []
    for kind in range(2):
        column = jnp.sum(leaf_ref[kind], axis=1, keepdims=True)
        lines.append(
            jnp.sum(jnp.where(spot == lane, column, 0.0), axis=0, keepdims=True)
        )
    tail = jnp.concatenate(lines + [jnp.zeros((SUB - 2, LANES), jnp.float32)], axis=0)
    hist_ref[own // 2 * LANES : own // 2 * LANES + SUB, :] = tail


def finish_kernel(
    total,
    hist_ref,
    path_ref,
    weight_ref,
    score_ref,
    hist3_ref,
    hist4_ref,
    value_ref,
    new_score_ref,
    new_weight_ref,
    weave_ref,
):
    own, tags, _ = hist4_ref.shape
    nodes4 = tags // 2
    nodes3 = nodes4 // 2
    leaves = value_ref.shape[1]
    for pair in range(own // 2):
        turned = hist_ref[pair * LANES : (pair + 1) * LANES, :].T
        for q in range(4):
            i = 2 * pair + q // 2
            h = q % 2
            lanes = slice(h * LANES, (h + 1) * LANES)
            start = q * tags
            keep = (pair * 4 + q) * tags

            def tag_rows(right, positive):
                first = start + right * 2 * nodes3 + positive * nodes3
                return turned[first : first + nodes3, :]

            sums = [tag_rows(r, 1) + tag_rows(r, 0) for r in range(2)]
            diffs = [tag_rows(r, 1) - tag_rows(r, 0) for r in range(2)]
            hist3_ref[i, 0:nodes3, lanes] = sums[0] + sums[1]
            hist3_ref[i, nodes3 : 2 * nodes3, lanes] = diffs[0] + diffs[1]
            for r in range(2):
                weave_ref[pl.ds(keep + r, nodes3, stride=2), :] = sums[r]
                weave_ref[pl.ds(keep + nodes4 + r, nodes3, stride=2), :] = diffs[r]
            hist4_ref[i, :, lanes] = weave_ref[keep : keep + tags, :]
    leaf_base = own // 2 * LANES
    pieces = hist_ref[leaf_base : leaf_base + SUB, :]
    lane = lax.broadcasted_iota(jnp.int32, (1, LANES), 1)
    full = pieces[0:1, :]
    rounded = pieces[1:2, :]
    other = pltpu.roll(rounded, LANES - leaves, 1)
    values = (other - rounded) / (other + rounded + 1.0)
    value_ref[...] = values[:, 0:leaves]
    negative = lane < leaves
    both = jnp.where(negative, values, pltpu.roll(values, leaves, 1))
    both = jnp.where(lane < 2 * leaves, both, 0.0)
    growth = jnp.exp(jnp.where(negative, both, -both))
    grand = jnp.sum(full * growth, axis=1, keepdims=True)
    factor = growth * (total / grand)
    factor8 = jnp.broadcast_to(factor, (SUB, LANES))
    both8 = jnp.broadcast_to(both, (SUB, LANES))
    for step in range(path_ref.shape[0] // SUB):
        rows = slice(step * SUB, (step + 1) * SUB)
        path = path_ref[rows, :]
        scale = jnp.take_along_axis(factor8, path, axis=1)
        shift = jnp.take_along_axis(both8, path, axis=1)
        new_weight_ref[rows, :] = weight_ref[rows, :] * scale
        new_score_ref[rows, :] = score_ref[rows, :] + shift


def combine_rows(part, axis, size):
    if size & (size - 1):
        return lax.psum(part, axis)
    reach = 1
    while reach < size:
        pairs = [(i, i ^ reach) for i in range(size)]
        part = part + lax.ppermute(part, axis, pairs)
        reach *= 2
    return part


def whole(memory=pltpu.VMEM):
    return pl.BlockSpec(memory_space=memory)


def on_device(
    row_parts,
    feat_parts,
    bin_codes,
    node_ids,
    labels,
    weights,
    predictions,
    level3_feature,
    level3_bin,
    level4_feature,
    level4_bin,
):
    features, row_count = bin_codes.shape
    groups = row_count // LANES
    own = features // feat_parts
    nodes3 = level3_feature.shape[0]
    nodes4 = level4_feature.shape[0]
    leaves = 2 * nodes4
    tags = 2 * nodes4
    codes = (
        bin_codes.reshape(features // SUB, SUB, groups, LANES)
        .transpose(0, 2, 1, 3)
        .reshape(features * groups, LANES)
    )
    square = (groups, LANES)
    node_sq = node_ids.reshape(square)
    label_sq = labels.reshape(square)
    weight_sq = weights.reshape(square)
    score_sq = predictions.reshape(square)
    hist_rows = own // 2 * LANES + SUB
    f32, i32 = jnp.float32, jnp.int32
    held = functools.partial(pltpu.with_memory_space_constraint, memory_space=pltpu.HBM)
    hist, path = pl.pallas_call(
        grow_kernel,
        out_shape=(pltpu.VMEM((hist_rows, LANES), f32), pltpu.VMEM(square, i32)),
        in_specs=[whole(pltpu.HBM)] * 8,
        out_specs=(whole(), whole()),
        scratch_shapes=[
            pltpu.SMEM((nodes3,), i32),
            pltpu.SMEM((nodes3,), i32),
            pltpu.SMEM((nodes4,), i32),
            pltpu.SMEM((nodes4,), i32),
            pltpu.VMEM(codes.shape, i32),
            pltpu.VMEM(square, i32),
            pltpu.VMEM(square, f32),
            pltpu.VMEM(square, f32),
            pltpu.VMEM((own, *square), i32),
            pltpu.VMEM((own, *square), i32),
            pltpu.VMEM(square, f32),
            pltpu.VMEM((own, LANES, 2 * tags), f32),
            pltpu.VMEM((2, 2 * leaves, LANES), f32),
            pltpu.SemaphoreType.DMA((8,)),
        ],
        compiler_params=pltpu.CompilerParams(vmem_limit_bytes=24 * 1024 * 1024),
    )(
        held(level3_feature),
        held(level3_bin),
        held(level4_feature),
        held(level4_bin),
        held(codes),
        held(node_sq),
        held(label_sq),
        held(weight_sq),
    )
    hist = combine_rows(hist, "rows", row_parts)
    hist3, hist4, values, new_scores, new_weights = pl.pallas_call(
        functools.partial(finish_kernel, float(row_count * row_parts)),
        out_shape=(
            jax.ShapeDtypeStruct((own, 2 * nodes3, BINS), f32),
            jax.ShapeDtypeStruct((own, 2 * nodes4, BINS), f32),
            jax.ShapeDtypeStruct((1, leaves), f32),
            jax.ShapeDtypeStruct(square, f32),
            jax.ShapeDtypeStruct(square, f32),
        ),
        in_specs=[whole()] * 4,
        out_specs=(whole(),) * 5,
        scratch_shapes=[pltpu.VMEM((own * 2 * tags, LANES), f32)],
        compiler_params=pltpu.CompilerParams(vmem_limit_bytes=24 * 1024 * 1024),
    )(hist, path, weight_sq, score_sq)
    return (
        hist3,
        hist4,
        values.reshape(leaves),
        new_scores.reshape(row_count),
        new_weights.reshape(row_count),
    )


def solution(mesh):
    placed = (P(None, "rows"), P("rows"), P("rows"), P("rows"), P("rows"), P(), P(), P(), P())
    return jax.shard_map(
        functools.partial(on_device, mesh.shape["rows"], mesh.shape["feat"]),
        mesh=mesh,
        in_specs=placed,
        out_specs=(P("feat", None, None), P("feat", None, None), P(), P("rows"), P("rows")),
        check_vma=False,
    )
```

time: 37.9 us -> 28.7 us (0.76)
  Pallas kernels: 13 us -> 8.59 us
  local copies, waits for them, and re-layouts: 4.36 us -> 0.01 us
    pallas_call x1, Pallas kernels: 12 us -> 7.57 us  [on_device(): pl.pallas_call(grow_kernel, out_shape=(pltpu.VMEM((hist_rows, LANES), f32...]
    unnamed x18 -> x4, local copies, waits for them, and re-layouts: 4.36 us -> 0.01 us
where the time goes in v2:
time: 28.7 us; the launch traced here: 28.5 us
  waiting for transfers between devices  11.4 us (40%)
  Pallas kernels  8.59 us (30%)
  starting transfers between devices  7.77 us (27%)
  between operations  0.68 us (2%)
    ppermute x3, waiting for transfers between devices, combine_rows(): part = part + lax.ppermute(part, axis, pairs)  11.4 us
    ppermute x3, starting transfers between devices, combine_rows(): part = part + lax.ppermute(part, axis, pairs)  7.77 us
    pallas_call x1, Pallas kernels, on_device(): pl.pallas_call(grow_kernel, out_shape=(pltpu.VMEM((hist_rows, LANES), f32...  7.57 us
    pallas_call x1, Pallas kernels, on_device(): pl.pallas_call(functools.partial(finish_kernel, float(row_count * row_par...  1.02 us
  transfers between devices with their start and end apart: 3, of which 3 were waited for; matrix products, arithmetic and copies ran while one was open for 0% of the time, Pallas kernels for 0%

profile of v2, /device:TPU:0, one launch (start us, length us, event | category | flops | bytes accessed | tf_op | source)
XLA Modules:
  0.0 28.5 jit_solution(17719359076999387662)
XLA Ops:
  0.6 7.6 %shard_map.128 = (f32[264,128]{1,0:T(8,128)S(1)}, s32[120,128]{1,0:T(8,128)S(1)}) custom-call(s32[8]{0:T(128)} %f3_hbm.1, s32[8]{0:T(128)} %b3_hbm.1, s32[16]{0:T(128)} %f4_hbm.1, s32[16]{0:T(128)} %b4_hbm.1, s32[1920,128]{1,0:T(8,128)} %bitcast.15, s32[120,128]{1,0:T(8,128)} %bitcast.16, f32[120,128]{1,0:T(8,128)} %bitcast.17, f32[120,128]{1,0:T(8,128)} %bitcast.12), custom_call_target="tpu_custom_call" | custom-call | tf_op jit(solution)/shard_map/pallas_call | solution.py:290
  8.2 3.0 %collective-permute-start = (f32[264,128]{1,0:T(8,128)S(1)}, f32[264,128]{1,0:T(8,128)S(1)}, u32[]{:S(2)}, u32[]{:S(2)}) collective-permute-start(f32[264,128]{1,0:T(8,128)S(1)} %get-tuple-element.12), channel_id=1, source_target_pairs={{0,4},{4,0},{8,12},{12,8},{16,20},{20,16},{24,28},{28,24},{1,5},{5... | collective-permute-start | bytes 405512 | tf_op jit(solution)/shard_map/ppermute | solution.py:248
  11.2 3.6 %collective-permute-done = f32[264,128]{1,0:T(8,128)S(1)} collective-permute-done((f32[264,128]{1,0:T(8,128)S(1)}, f32[264,128]{1,0:T(8,128)S(1)}, u32[]{:S(2)}, u32[]{:S(2)}) %collective-permute-start) | collective-permute-done | bytes 135200 | tf_op jit(solution)/shard_map/ppermute | solution.py:248
  14.8 1.9 %collective-permute-start.1 = (f32[264,128]{1,0:T(8,128)S(1)}, f32[264,128]{1,0:T(8,128)S(1)}, u32[]{:S(2)}, u32[]{:S(2)}) collective-permute-start(f32[264,128]{1,0:T(8,128)S(1)} %add.9), channel_id=1, source_target_pairs={{0,8},{4,12},{8,0},{12,4},{16,24},{20,28},{24,16},{28,20},{1,9},{5... | collective-permute-start | bytes 405512 | tf_op jit(solution)/shard_map/ppermute | solution.py:248
  16.7 3.2 %collective-permute-done.1 = f32[264,128]{1,0:T(8,128)S(1)} collective-permute-done((f32[264,128]{1,0:T(8,128)S(1)}, f32[264,128]{1,0:T(8,128)S(1)}, u32[]{:S(2)}, u32[]{:S(2)}) %collective-permute-start.1) | collective-permute-done | bytes 135200 | tf_op jit(solution)/shard_map/ppermute | solution.py:248
  19.9 0.0 copy-start
  20.0 0.0 copy-start.1
  20.0 2.9 %collective-permute-start.2 = (f32[264,128]{1,0:T(8,128)S(1)}, f32[264,128]{1,0:T(8,128)S(1)}, u32[]{:S(2)}, u32[]{:S(2)}) collective-permute-start(f32[264,128]{1,0:T(8,128)S(1)} %add.10), channel_id=1, source_target_pairs={{0,16},{4,20},{8,24},{12,28},{16,0},{20,4},{24,8},{28,12},{1,17},{... | collective-permute-start | bytes 405512 | tf_op jit(solution)/shard_map/ppermute | solution.py:248
  22.8 4.6 %collective-permute-done.2 = f32[264,128]{1,0:T(8,128)S(1)} collective-permute-done((f32[264,128]{1,0:T(8,128)S(1)}, f32[264,128]{1,0:T(8,128)S(1)}, u32[]{:S(2)}, u32[]{:S(2)}) %collective-permute-start.2) | collective-permute-done | bytes 135200 | tf_op jit(solution)/shard_map/ppermute | solution.py:248
  27.5 0.0 copy-done
  27.5 0.0 copy-done.1
  27.5 1.0 %shard_map.129 = (f32[4,16,256]{2,1,0:T(8,128)}, f32[4,32,256]{2,1,0:T(8,128)}, f32[1,32]{1,0:T(1,128)}, f32[120,128]{1,0:T(8,128)}, f32[120,128]{1,0:T(8,128)}) custom-call(f32[264,128]{1,0:T(8,128)S(1)} %add.11.hist_ref, s32[120,128]{1,0:T(8,128)S(1)} %get-tuple-element.13.path_ref, f32[120,128]{1,0:T(8,128)S(1)} %bitcast.13, f32[120,128]{1,0:T(8,128)S(1)} %bitcast.14), custom_call_target="tpu_custom_call" | custom-call | tf_op jit(solution)/shard_map/pallas_call | solution.py:323
  (3 shorter events, 0.1 us)
Async XLA Ops:
  8.2 6.6 %collective-permute-start = (f32[264,128]{1,0:T(8,128)S(1)}, f32[264,128]{1,0:T(8,128)S(1)}, u32[]{:S(2)}, u32[]{:S(2)}) collective-permute-start(f32[264,128]{1,0:T(8,128)S(1)} %get-tuple-element.12), channel_id=1, source_target_pairs={{0,4},{4,0},{8,12},{12,8},{16,20},{20,16},{24,28},{28,24},{1,5},{5... | collective-permute-start | bytes 405512 | tf_op jit(solution)/shard_map/ppermute | solution.py:248
  14.8 5.1 %collective-permute-start.1 = (f32[264,128]{1,0:T(8,128)S(1)}, f32[264,128]{1,0:T(8,128)S(1)}, u32[]{:S(2)}, u32[]{:S(2)}) collective-permute-start(f32[264,128]{1,0:T(8,128)S(1)} %add.9), channel_id=1, source_target_pairs={{0,8},{4,12},{8,0},{12,4},{16,24},{20,28},{24,16},{28,20},{1,9},{5... | collective-permute-start | bytes 405512 | tf_op jit(solution)/shard_map/ppermute | solution.py:248
  19.9 7.5 %copy-start = (f32[15360]{0:T(1024)S(1)}, f32[15360]{0:T(1024)}, u32[]{:S(2)}) copy-start(f32[15360]{0:T(1024)} %param.12) | copy-start | bytes 184324
  20.0 7.5 %copy-start.1 = (f32[15360]{0:T(1024)S(1)}, f32[15360]{0:T(1024)}, u32[]{:S(2)}) copy-start(f32[15360]{0:T(1024)} %param.13) | copy-start | bytes 184324
  20.0 7.5 %collective-permute-start.2 = (f32[264,128]{1,0:T(8,128)S(1)}, f32[264,128]{1,0:T(8,128)S(1)}, u32[]{:S(2)}, u32[]{:S(2)}) collective-permute-start(f32[264,128]{1,0:T(8,128)S(1)} %add.10), channel_id=1, source_target_pairs={{0,16},{4,20},{8,24},{12,28},{16,0},{20,4},{24,8},{28,12},{1,17},{... | collective-permute-start | bytes 405512 | tf_op jit(solution)/shard_map/ppermute | solution.py:248

commit v3 on v2

--- a/solution.py
+++ b/solution.py
@@ -124,7 +124,7 @@
         parts = [jnp.where(value == ranks[g], filled, nothing) for g in range(count // (2 * SUB))]
         return jnp.concatenate(parts, axis=0)
 
-    span = next(n for n in (24, 16, 8) if groups % n == 0)
+    span = next(n for n in (120, 24, 16, 8) if groups % n == 0)
 
     def tally(turn, carry):
         base = turn * span
@@ -239,15 +239,22 @@
         new_score_ref[rows, :] = score_ref[rows, :] + shift
 
 
-def combine_rows(part, axis, size):
-    if size & (size - 1):
-        return lax.psum(part, axis)
-    reach = 1
-    while reach < size:
-        pairs = [(i, i ^ reach) for i in range(size)]
-        part = part + lax.ppermute(part, axis, pairs)
-        reach *= 2
+def combine_rows(part, row_parts, feat_parts):
+    if row_parts & (row_parts - 1):
+        return lax.psum(part, "rows")
+    bits = row_parts.bit_length() - 1
+    for step in range(bits):
+        pairs = []
+        for row in range(row_parts):
+            for feat in range(feat_parts):
+                other = row ^ reach(feat, step, bits)
+                pairs.append((row * feat_parts + feat, other * feat_parts + feat))
+        part = part + lax.ppermute(part, ("rows", "feat"), pairs)
     return part
+
+
+def reach(feat, step, bits):
+    return 1 << (step + feat % 2 * (bits - 1)) % bits
 
 
 def whole(memory=pltpu.VMEM):
@@ -319,7 +326,7 @@
         held(label_sq),
         held(weight_sq),
     )
-    hist = combine_rows(hist, "rows", row_parts)
+    hist = combine_rows(hist, row_parts, feat_parts)
     hist3, hist4, values, new_scores, new_weights = pl.pallas_call(
         functools.partial(finish_kernel, float(row_count * row_parts)),
         out_shape=(

time: 28.7 us -> 26.1 us (0.909)
  waiting for transfers between devices: 11.4 us -> 9.09 us
  Pallas kernels: 8.59 us -> 7.74 us
  starting transfers between devices: 7.77 us -> 8.28 us
    ppermute x3, waiting for transfers between devices: 11.4 us -> 9.09 us  [combine_rows(): part = part + lax.ppermute(part, ('rows', 'feat'), pairs)]
    pallas_call x1, Pallas kernels: 7.57 us -> 6.72 us  [on_device(): pl.pallas_call(grow_kernel, out_shape=(pltpu.VMEM((hist_rows, LANES), f32...]
    ppermute x3, starting transfers between devices: 7.77 us -> 8.28 us  [combine_rows(): part = part + lax.ppermute(part, ('rows', 'feat'), pairs)]
where the time goes in v3:
time: 26.1 us; the launch traced here: 25.9 us
  waiting for transfers between devices  9.09 us (35%)
  starting transfers between devices  8.28 us (32%)
  Pallas kernels  7.74 us (30%)
  between operations  0.68 us (3%)
    ppermute x3, waiting for transfers between devices, combine_rows(): part = part + lax.ppermute(part, ('rows', 'feat'), pairs)  9.09 us
    ppermute x3, starting transfers between devices, combine_rows(): part = part + lax.ppermute(part, ('rows', 'feat'), pairs)  8.28 us
    pallas_call x1, Pallas kernels, on_device(): pl.pallas_call(grow_kernel, out_shape=(pltpu.VMEM((hist_rows, LANES), f32...  6.72 us
    pallas_call x1, Pallas kernels, on_device(): pl.pallas_call(functools.partial(finish_kernel, float(row_count * row_par...  1.02 us
  transfers between devices with their start and end apart: 3, of which 3 were waited for; matrix products, arithmetic and copies ran while one was open for 0% of the time, Pallas kernels for 0%

profile of v3, /device:TPU:0, one launch (start us, length us, event | category | flops | bytes accessed | tf_op | source)
XLA Modules:
  0.0 25.9 jit_solution(13777193640283628014)
XLA Ops:
  0.6 6.7 %shard_map.128 = (f32[264,128]{1,0:T(8,128)S(1)}, s32[120,128]{1,0:T(8,128)S(1)}) custom-call(s32[8]{0:T(128)} %f3_hbm.1, s32[8]{0:T(128)} %b3_hbm.1, s32[16]{0:T(128)} %f4_hbm.1, s32[16]{0:T(128)} %b4_hbm.1, s32[1920,128]{1,0:T(8,128)} %bitcast.15, s32[120,128]{1,0:T(8,128)} %bitcast.16, f32[120,128]{1,0:T(8,128)} %bitcast.17, f32[120,128]{1,0:T(8,128)} %bitcast.12), custom_call_target="tpu_custom_call" | custom-call | tf_op jit(solution)/shard_map/pallas_call | solution.py:297
  7.4 3.0 %collective-permute-start = (f32[264,128]{1,0:T(8,128)S(1)}, f32[264,128]{1,0:T(8,128)S(1)}, u32[]{:S(2)}, u32[]{:S(2)}) collective-permute-start(f32[264,128]{1,0:T(8,128)S(1)} %get-tuple-element.12), channel_id=1, source_target_pairs={{0,4},{1,17},{2,6},{3,19},{4,0},{5,21},{6,2},{7,23},{8,12},{9,25},... | collective-permute-start | bytes 405512 | tf_op jit(solution)/shard_map/ppermute | solution.py:252
  10.4 3.0 %collective-permute-done = f32[264,128]{1,0:T(8,128)S(1)} collective-permute-done((f32[264,128]{1,0:T(8,128)S(1)}, f32[264,128]{1,0:T(8,128)S(1)}, u32[]{:S(2)}, u32[]{:S(2)}) %collective-permute-start) | collective-permute-done | bytes 135200 | tf_op jit(solution)/shard_map/ppermute | solution.py:252
  13.4 2.1 %collective-permute-start.1 = (f32[264,128]{1,0:T(8,128)S(1)}, f32[264,128]{1,0:T(8,128)S(1)}, u32[]{:S(2)}, u32[]{:S(2)}) collective-permute-start(f32[264,128]{1,0:T(8,128)S(1)} %add.9), channel_id=1, source_target_pairs={{0,8},{1,5},{2,10},{3,7},{4,12},{5,1},{6,14},{7,3},{8,0},{9,13},{1... | collective-permute-start | bytes 405512 | tf_op jit(solution)/shard_map/ppermute | solution.py:252
  15.6 3.0 %collective-permute-done.1 = f32[264,128]{1,0:T(8,128)S(1)} collective-permute-done((f32[264,128]{1,0:T(8,128)S(1)}, f32[264,128]{1,0:T(8,128)S(1)}, u32[]{:S(2)}, u32[]{:S(2)}) %collective-permute-start.1) | collective-permute-done | bytes 135200 | tf_op jit(solution)/shard_map/ppermute | solution.py:252
  18.6 0.0 copy-start
  18.6 0.0 copy-start.1
  18.6 3.1 %collective-permute-start.2 = (f32[264,128]{1,0:T(8,128)S(1)}, f32[264,128]{1,0:T(8,128)S(1)}, u32[]{:S(2)}, u32[]{:S(2)}) collective-permute-start(f32[264,128]{1,0:T(8,128)S(1)} %add.10), channel_id=1, source_target_pairs={{0,16},{1,9},{2,18},{3,11},{4,20},{5,13},{6,22},{7,15},{8,24},{9,1... | collective-permute-start | bytes 405512 | tf_op jit(solution)/shard_map/ppermute | solution.py:252
  21.7 3.1 %collective-permute-done.2 = f32[264,128]{1,0:T(8,128)S(1)} collective-permute-done((f32[264,128]{1,0:T(8,128)S(1)}, f32[264,128]{1,0:T(8,128)S(1)}, u32[]{:S(2)}, u32[]{:S(2)}) %collective-permute-start.2) | collective-permute-done | bytes 135200 | tf_op jit(solution)/shard_map/ppermute | solution.py:252
  24.8 0.0 copy-done
  24.8 0.0 copy-done.1
  24.8 1.0 %shard_map.129 = (f32[4,16,256]{2,1,0:T(8,128)}, f32[4,32,256]{2,1,0:T(8,128)}, f32[1,32]{1,0:T(1,128)}, f32[120,128]{1,0:T(8,128)}, f32[120,128]{1,0:T(8,128)}) custom-call(f32[264,128]{1,0:T(8,128)S(1)} %add.11.hist_ref, s32[120,128]{1,0:T(8,128)S(1)} %get-tuple-element.13.path_ref, f32[120,128]{1,0:T(8,128)S(1)} %bitcast.13, f32[120,128]{1,0:T(8,128)S(1)} %bitcast.14), custom_call_target="tpu_custom_call" | custom-call | tf_op jit(solution)/shard_map/pallas_call | solution.py:330
  (3 shorter events, 0.1 us)
Async XLA Ops:
  7.4 6.0 %collective-permute-start = (f32[264,128]{1,0:T(8,128)S(1)}, f32[264,128]{1,0:T(8,128)S(1)}, u32[]{:S(2)}, u32[]{:S(2)}) collective-permute-start(f32[264,128]{1,0:T(8,128)S(1)} %get-tuple-element.12), channel_id=1, source_target_pairs={{0,4},{1,17},{2,6},{3,19},{4,0},{5,21},{6,2},{7,23},{8,12},{9,25},... | collective-permute-start | bytes 405512 | tf_op jit(solution)/shard_map/ppermute | solution.py:252
  13.4 5.1 %collective-permute-start.1 = (f32[264,128]{1,0:T(8,128)S(1)}, f32[264,128]{1,0:T(8,128)S(1)}, u32[]{:S(2)}, u32[]{:S(2)}) collective-permute-start(f32[264,128]{1,0:T(8,128)S(1)} %add.9), channel_id=1, source_target_pairs={{0,8},{1,5},{2,10},{3,7},{4,12},{5,1},{6,14},{7,3},{8,0},{9,13},{1... | collective-permute-start | bytes 405512 | tf_op jit(solution)/shard_map/ppermute | solution.py:252
  18.6 6.3 %copy-start = (f32[15360]{0:T(1024)S(1)}, f32[15360]{0:T(1024)}, u32[]{:S(2)}) copy-start(f32[15360]{0:T(1024)} %param.12) | copy-start | bytes 184324
  18.6 6.3 %copy-start.1 = (f32[15360]{0:T(1024)S(1)}, f32[15360]{0:T(1024)}, u32[]{:S(2)}) copy-start(f32[15360]{0:T(1024)} %param.13) | copy-start | bytes 184324
  18.6 6.2 %collective-permute-start.2 = (f32[264,128]{1,0:T(8,128)S(1)}, f32[264,128]{1,0:T(8,128)S(1)}, u32[]{:S(2)}, u32[]{:S(2)}) collective-permute-start(f32[264,128]{1,0:T(8,128)S(1)} %add.10), channel_id=1, source_target_pairs={{0,16},{1,9},{2,18},{3,11},{4,20},{5,13},{6,22},{7,15},{8,24},{9,1... | collective-permute-start | bytes 405512 | tf_op jit(solution)/shard_map/ppermute | solution.py:252

commit v4 on v3

--- a/solution.py
+++ b/solution.py
@@ -10,6 +10,7 @@
 BINS = 256
 LANES = 128
 SUB = 8
+DEPTH = 256
 NT = (((1,), (1,)), ((), ()))
 
 
@@ -35,8 +36,7 @@
     low_ref,
     slot_ref,
     high_ref,
-    sums_ref,
-    leaf_ref,
+    piece_ref,
     sems,
 ):
     groups = node_ref.shape[0]
@@ -45,7 +45,6 @@
     nodes3 = f3_ref.shape[0]
     nodes4 = f4_ref.shape[0]
     tag_count = 2 * nodes4
-    paths = 4 * nodes4
     moves = [
         pltpu.make_async_copy(source, target, sems.at[i])
         for i, (source, target) in enumerate(
@@ -63,8 +62,7 @@
     ]
     for move in moves:
         move.start()
-    sums_ref[...] = jnp.zeros_like(sums_ref)
-    leaf_ref[...] = jnp.zeros_like(leaf_ref)
+    piece_ref[...] = jnp.zeros_like(piece_ref)
     for move in moves:
         move.wait()
 
@@ -96,12 +94,19 @@
         rows = rows_of(step)
         positive = jnp.where(label_ref[rows, :] > 0, 1, 0)
         tag = right3[step] * (2 * nodes3) + positive * nodes3 + node3[step]
-        path_ref[rows, :] = positive * (2 * nodes4) + 2 * node4[step] + right4[step]
+        path_ref[rows, :] = right4[step] * tag_count + tag
         for i in range(own):
             code = code_block(starts[i], step)
             low_ref[i, rows, :] = code & (LANES - 1)
             slot_ref[i, rows, :] = (code // LANES) * tag_count + tag
-        high_ref[rows, :] = weight_ref[rows, :].astype(jnp.bfloat16).astype(jnp.float32)
+        weight = weight_ref[rows, :]
+        high = weight.astype(jnp.bfloat16).astype(jnp.float32)
+        mid = (weight - high).astype(jnp.bfloat16).astype(jnp.float32)
+        high_ref[rows, :] = high
+        for k, piece in enumerate((high, mid, weight - high - mid)):
+            for side in range(2):
+                spots = pl.ds(step * (SUB * SUB) + 2 * k + side, SUB, stride=SUB)
+                piece_ref[spots, :] = jnp.where(right4[step] == side, piece, 0.0)
 
     cell = (2 * SUB, LANES)
     iota = lax.broadcasted_iota(jnp.int32, cell, 0)
@@ -109,71 +114,70 @@
     ranks = [(iota + 2 * SUB * g).astype(small) for g in range(LANES // (2 * SUB))]
     one = jnp.ones(cell, jnp.bfloat16)
     nothing = jnp.zeros(cell, jnp.bfloat16)
-    leaf_rank = [
-        lax.broadcasted_iota(jnp.int32, (SUB, LANES), 0) + SUB * g for g in range(paths // SUB)
-    ]
-
     def spread(ref, row, dtype, *lead):
         line = ref[(*lead, pl.ds(row, 1), slice(None))]
         return jnp.broadcast_to(line, cell).astype(dtype)
 
-    def wide(ref, row):
-        return jnp.broadcast_to(ref[pl.ds(row, 1), :], (SUB, LANES))
-
     def onehot(value, count, filled):
         parts = [jnp.where(value == ranks[g], filled, nothing) for g in range(count // (2 * SUB))]
         return jnp.concatenate(parts, axis=0)
 
-    span = next(n for n in (120, 24, 16, 8) if groups % n == 0)
-
-    def tally(turn, carry):
-        base = turn * span
-        lines = range(span)
-        heavy = [spread(high_ref, base + k, jnp.bfloat16) for k in lines]
-        for i in range(own):
-            slots = jnp.concatenate(
+    halves = DEPTH // LANES
+    tiles = groups // halves
+    units = 2
+
+    def fill(tile):
+        lines = range(tile * halves, (tile + 1) * halves)
+        columns = [
+            jnp.concatenate(
                 [
-                    onehot(spread(slot_ref, base + k, small, i), 2 * tag_count, heavy[k])
-                    for k in lines
+                    onehot(spread(slot_ref, line, small, i), 2 * tag_count, one)
+                    for i in range(own)
                 ],
-                axis=1,
+                axis=0,
             )
-            lows = jnp.concatenate(
-                [onehot(spread(low_ref, base + k, small, i), LANES, one) for k in lines],
-                axis=1,
+            for line in lines
+        ]
+        pltpu.matmul_push_rhs(
+            jnp.concatenate(columns, axis=1), tile // units % 2, tile % units, transpose=True
+        )
+
+    def stream(tile, accs):
+        columns = []
+        for line in range(tile * halves, (tile + 1) * halves):
+            heavy = spread(high_ref, line, jnp.bfloat16)
+            parts = [onehot(spread(low_ref, line, small, i), LANES, heavy) for i in range(own)]
+            pieces = piece_ref[line * SUB : (line + 1) * SUB, :]
+            parts.append(
+                jnp.concatenate([pieces, jnp.zeros_like(pieces)], axis=0).astype(jnp.bfloat16)
             )
-            sums_ref[i] += lax.dot_general(lows, slots, NT, preferred_element_type=jnp.float32)
-        count = paths // SUB
-        exact = [leaf_ref[0, rows_of(g), :] for g in range(count)]
-        rounded = [leaf_ref[1, rows_of(g), :] for g in range(count)]
-        for k in lines:
-            path = wide(path_ref, base + k)
-            weight = wide(weight_ref, base + k)
-            high = wide(high_ref, base + k)
-            for g in range(count):
-                here = path == leaf_rank[g]
-                exact[g] += jnp.where(here, weight, 0.0)
-                rounded[g] += jnp.where(here, high, 0.0)
-        for g in range(count):
-            leaf_ref[0, rows_of(g), :] = exact[g]
-            leaf_ref[1, rows_of(g), :] = rounded[g]
-        return carry
-
-    lax.fori_loop(0, groups // span, tally, 0)
-    for i in range(own // 2):
-        hist_ref[i * LANES : (i + 1) * LANES, :] = jnp.concatenate(
-            [sums_ref[2 * i], sums_ref[2 * i + 1]], axis=1
-        )
-    spot = lax.broadcasted_iota(jnp.int32, (paths, LANES), 0)
-    lane = lax.broadcasted_iota(jnp.int32, (paths, LANES), 1)
-    lines = []
-    for kind in range(2):
-        column = jnp.sum(leaf_ref[kind], axis=1, keepdims=True)
-        lines.append(
-            jnp.sum(jnp.where(spot == lane, column, 0.0), axis=0, keepdims=True)
-        )
-    tail = jnp.concatenate(lines + [jnp.zeros((SUB - 2, LANES), jnp.float32)], axis=0)
-    hist_ref[own // 2 * LANES : own // 2 * LANES + SUB, :] = tail
+            columns.append(jnp.concatenate(parts, axis=0))
+        pltpu.matmul_acc_lhs(
+            accs[tile % units], jnp.concatenate(columns, axis=1), tile // units % 2
+        )
+
+    def product(*accs):
+        for tile in range(units):
+            fill(tile)
+        for tile in range(tiles):
+            if tile + units < tiles:
+                fill(tile + units)
+            stream(tile, accs)
+        return pltpu.matmul_pop(accs[0]) + pltpu.matmul_pop(accs[1])
+
+    shape = (own * LANES + 2 * SUB, DEPTH)
+    sums = pl.run_scoped(
+        product, *(pltpu.ACC(unit)(shape, jnp.float32) for unit in range(units))
+    )
+    left = lax.broadcasted_iota(jnp.int32, (LANES, LANES), 1) < 2 * tag_count
+    for pair in range(own // 2):
+        lanes = slice(pair * LANES, (pair + 1) * LANES)
+        rows = [slice(i * LANES, (i + 1) * LANES) for i in (2 * pair, 2 * pair + 1)]
+        hist_ref[lanes, :] = jnp.where(left, sums[rows[0], lanes], sums[rows[1], lanes])
+    doubled = sums[own * LANES : own * LANES + SUB, 0:LANES]
+    hist_ref[own // 2 * LANES : own // 2 * LANES + SUB, :] = doubled + pltpu.roll(
+        doubled, LANES - tag_count, 1
+    )
 
 
 def finish_kernel(
@@ -217,19 +221,33 @@
     leaf_base = own // 2 * LANES
     pieces = hist_ref[leaf_base : leaf_base + SUB, :]
     lane = lax.broadcasted_iota(jnp.int32, (1, LANES), 1)
-    full = pieces[0:1, :]
-    rounded = pieces[1:2, :]
-    other = pltpu.roll(rounded, LANES - leaves, 1)
-    values = (other - rounded) / (other + rounded + 1.0)
-    value_ref[...] = values[:, 0:leaves]
-    negative = lane < leaves
-    both = jnp.where(negative, values, pltpu.roll(values, leaves, 1))
-    both = jnp.where(lane < 2 * leaves, both, 0.0)
-    growth = jnp.exp(jnp.where(negative, both, -both))
-    grand = jnp.sum(full * growth, axis=1, keepdims=True)
+    right = (lane & tags) > 0
+    positive = (lane & nodes3) > 0
+
+    def both_sides(k):
+        return jnp.where(
+            right, pltpu.roll(pieces[2 * k + 1 : 2 * k + 2, :], tags, 1), pieces[2 * k : 2 * k + 1, :]
+        )
+
+    def partner(line):
+        return jnp.where(
+            positive, pltpu.roll(line, nodes3, 1), pltpu.roll(line, LANES - nodes3, 1)
+        )
+
+    rounded = both_sides(0)
+    full = rounded + (both_sides(1) + both_sides(2))
+    inside = lane < 2 * tags
+    other = partner(rounded)
+    gap = jnp.where(positive, rounded - other, other - rounded)
+    values = jnp.where(inside, gap / (rounded + other + 1.0), 0.0)
+    growth = jnp.exp(jnp.where(positive, -values, values))
+    grand = jnp.sum(jnp.where(inside, full * growth, 0.0), axis=1, keepdims=True)
     factor = growth * (total / grand)
     factor8 = jnp.broadcast_to(factor, (SUB, LANES))
-    both8 = jnp.broadcast_to(both, (SUB, LANES))
+    both8 = jnp.broadcast_to(values, (SUB, LANES))
+    leaf = lax.broadcasted_iota(jnp.int32, (SUB, LANES), 1)
+    spot = (leaf & 1) * tags + ((leaf >> 1) & 1) * (2 * nodes3) + ((leaf >> 2) & (nodes3 - 1))
+    value_ref[...] = jnp.take_along_axis(both8, spot, axis=1)[0:1, 0:leaves]
     for step in range(path_ref.shape[0] // SUB):
         rows = slice(step * SUB, (step + 1) * SUB)
         path = path_ref[rows, :]
@@ -311,8 +329,7 @@
             pltpu.VMEM((own, *square), i32),
             pltpu.VMEM((own, *square), i32),
             pltpu.VMEM(square, f32),
-            pltpu.VMEM((own, LANES, 2 * tags), f32),
-            pltpu.VMEM((2, 2 * leaves, LANES), f32),
+            pltpu.VMEM((groups * SUB, LANES), f32),
             pltpu.SemaphoreType.DMA((8,)),
         ],
         compiler_params=pltpu.CompilerParams(vmem_limit_bytes=24 * 1024 * 1024),

time: 26.1 us -> 25.3 us (0.969)
  Pallas kernels: 7.74 us -> 6.98 us
    pallas_call x1, Pallas kernels: 6.72 us -> 5.97 us  [on_device(): pl.pallas_call(grow_kernel, out_shape=(pltpu.VMEM((hist_rows, LANES), f32...]
where the time goes in v4:
time: 25.3 us; the launch traced here: 25.1 us
  waiting for transfers between devices  9.09 us (36%)
  starting transfers between devices  8.27 us (33%)
  Pallas kernels  6.98 us (28%)
  between operations  0.68 us (3%)
    ppermute x3, waiting for transfers between devices, combine_rows(): part = part + lax.ppermute(part, ('rows', 'feat'), pairs)  9.09 us
    ppermute x3, starting transfers between devices, combine_rows(): part = part + lax.ppermute(part, ('rows', 'feat'), pairs)  8.27 us
    pallas_call x1, Pallas kernels, on_device(): pl.pallas_call(grow_kernel, out_shape=(pltpu.VMEM((hist_rows, LANES), f32...  5.97 us
    pallas_call x1, Pallas kernels, on_device(): pl.pallas_call(functools.partial(finish_kernel, float(row_count * row_par...  1 us
  transfers between devices with their start and end apart: 3, of which 3 were waited for; matrix products, arithmetic and copies ran while one was open for 0% of the time, Pallas kernels for 0%

profile of v4, /device:TPU:0, one launch (start us, length us, event | category | flops | bytes accessed | tf_op | source)
XLA Modules:
  0.0 25.1 jit_solution(6866473515398628773)
XLA Ops:
  0.6 6.0 %shard_map.128 = (f32[264,128]{1,0:T(8,128)S(1)}, s32[120,128]{1,0:T(8,128)S(1)}) custom-call(s32[8]{0:T(128)} %f3_hbm.1, s32[8]{0:T(128)} %b3_hbm.1, s32[16]{0:T(128)} %f4_hbm.1, s32[16]{0:T(128)} %b4_hbm.1, s32[1920,128]{1,0:T(8,128)} %bitcast.15, s32[120,128]{1,0:T(8,128)} %bitcast.16, f32[120,128]{1,0:T(8,128)} %bitcast.17, f32[120,128]{1,0:T(8,128)} %bitcast.12), custom_call_target="tpu_custom_call" | custom-call | tf_op jit(solution)/shard_map/pallas_call | solution.py:315
  6.6 3.0 %collective-permute-start = (f32[264,128]{1,0:T(8,128)S(1)}, f32[264,128]{1,0:T(8,128)S(1)}, u32[]{:S(2)}, u32[]{:S(2)}) collective-permute-start(f32[264,128]{1,0:T(8,128)S(1)} %get-tuple-element.12), channel_id=1, source_target_pairs={{0,4},{1,17},{2,6},{3,19},{4,0},{5,21},{6,2},{7,23},{8,12},{9,25},... | collective-permute-start | bytes 405512 | tf_op jit(solution)/shard_map/ppermute | solution.py:270
  9.6 3.0 %collective-permute-done = f32[264,128]{1,0:T(8,128)S(1)} collective-permute-done((f32[264,128]{1,0:T(8,128)S(1)}, f32[264,128]{1,0:T(8,128)S(1)}, u32[]{:S(2)}, u32[]{:S(2)}) %collective-permute-start) | collective-permute-done | bytes 135200 | tf_op jit(solution)/shard_map/ppermute | solution.py:270
  12.7 2.1 %collective-permute-start.1 = (f32[264,128]{1,0:T(8,128)S(1)}, f32[264,128]{1,0:T(8,128)S(1)}, u32[]{:S(2)}, u32[]{:S(2)}) collective-permute-start(f32[264,128]{1,0:T(8,128)S(1)} %add.9), channel_id=1, source_target_pairs={{0,8},{1,5},{2,10},{3,7},{4,12},{5,1},{6,14},{7,3},{8,0},{9,13},{1... | collective-permute-start | bytes 405512 | tf_op jit(solution)/shard_map/ppermute | solution.py:270
  14.8 3.0 %collective-permute-done.1 = f32[264,128]{1,0:T(8,128)S(1)} collective-permute-done((f32[264,128]{1,0:T(8,128)S(1)}, f32[264,128]{1,0:T(8,128)S(1)}, u32[]{:S(2)}, u32[]{:S(2)}) %collective-permute-start.1) | collective-permute-done | bytes 135200 | tf_op jit(solution)/shard_map/ppermute | solution.py:270
  17.8 0.0 copy-start
  17.8 0.0 copy-start.1
  17.8 3.1 %collective-permute-start.2 = (f32[264,128]{1,0:T(8,128)S(1)}, f32[264,128]{1,0:T(8,128)S(1)}, u32[]{:S(2)}, u32[]{:S(2)}) collective-permute-start(f32[264,128]{1,0:T(8,128)S(1)} %add.10), channel_id=1, source_target_pairs={{0,16},{1,9},{2,18},{3,11},{4,20},{5,13},{6,22},{7,15},{8,24},{9,1... | collective-permute-start | bytes 405512 | tf_op jit(solution)/shard_map/ppermute | solution.py:270
  20.9 3.1 %collective-permute-done.2 = f32[264,128]{1,0:T(8,128)S(1)} collective-permute-done((f32[264,128]{1,0:T(8,128)S(1)}, f32[264,128]{1,0:T(8,128)S(1)}, u32[]{:S(2)}, u32[]{:S(2)}) %collective-permute-start.2) | collective-permute-done | bytes 135200 | tf_op jit(solution)/shard_map/ppermute | solution.py:270
  24.1 0.0 copy-done
  24.1 0.0 copy-done.1
  24.1 1.0 %shard_map.129 = (f32[4,16,256]{2,1,0:T(8,128)}, f32[4,32,256]{2,1,0:T(8,128)}, f32[1,32]{1,0:T(1,128)}, f32[120,128]{1,0:T(8,128)}, f32[120,128]{1,0:T(8,128)}) custom-call(f32[264,128]{1,0:T(8,128)S(1)} %add.11.hist_ref, s32[120,128]{1,0:T(8,128)S(1)} %get-tuple-element.13.path_ref, f32[120,128]{1,0:T(8,128)S(1)} %bitcast.13, f32[120,128]{1,0:T(8,128)S(1)} %bitcast.14), custom_call_target="tpu_custom_call" | custom-call | tf_op jit(solution)/shard_map/pallas_call | solution.py:347
  (3 shorter events, 0.1 us)
Async XLA Ops:
  6.6 6.0 %collective-permute-start = (f32[264,128]{1,0:T(8,128)S(1)}, f32[264,128]{1,0:T(8,128)S(1)}, u32[]{:S(2)}, u32[]{:S(2)}) collective-permute-start(f32[264,128]{1,0:T(8,128)S(1)} %get-tuple-element.12), channel_id=1, source_target_pairs={{0,4},{1,17},{2,6},{3,19},{4,0},{5,21},{6,2},{7,23},{8,12},{9,25},... | collective-permute-start | bytes 405512 | tf_op jit(solution)/shard_map/ppermute | solution.py:270
  12.7 5.1 %collective-permute-start.1 = (f32[264,128]{1,0:T(8,128)S(1)}, f32[264,128]{1,0:T(8,128)S(1)}, u32[]{:S(2)}, u32[]{:S(2)}) collective-permute-start(f32[264,128]{1,0:T(8,128)S(1)} %add.9), channel_id=1, source_target_pairs={{0,8},{1,5},{2,10},{3,7},{4,12},{5,1},{6,14},{7,3},{8,0},{9,13},{1... | collective-permute-start | bytes 405512 | tf_op jit(solution)/shard_map/ppermute | solution.py:270
  17.8 6.3 %copy-start = (f32[15360]{0:T(1024)S(1)}, f32[15360]{0:T(1024)}, u32[]{:S(2)}) copy-start(f32[15360]{0:T(1024)} %param.12) | copy-start | bytes 184324
  17.8 6.2 %copy-start.1 = (f32[15360]{0:T(1024)S(1)}, f32[15360]{0:T(1024)}, u32[]{:S(2)}) copy-start(f32[15360]{0:T(1024)} %param.13) | copy-start | bytes 184324
  17.8 6.2 %collective-permute-start.2 = (f32[264,128]{1,0:T(8,128)S(1)}, f32[264,128]{1,0:T(8,128)S(1)}, u32[]{:S(2)}, u32[]{:S(2)}) collective-permute-start(f32[264,128]{1,0:T(8,128)S(1)} %add.10), channel_id=1, source_target_pairs={{0,16},{1,9},{2,18},{3,11},{4,20},{5,13},{6,22},{7,15},{8,24},{9,1... | collective-permute-start | bytes 405512 | tf_op jit(solution)/shard_map/ppermute | solution.py:270

commit v5 on v4

--- a/solution.py
+++ b/solution.py
@@ -15,16 +15,6 @@
 
 
 def grow_kernel(
-    f3_hbm,
-    b3_hbm,
-    f4_hbm,
-    b4_hbm,
-    codes_hbm,
-    node_hbm,
-    label_hbm,
-    weight_hbm,
-    hist_ref,
-    path_ref,
     f3_ref,
     b3_ref,
     f4_ref,
@@ -33,11 +23,12 @@
     node_ref,
     label_ref,
     weight_ref,
+    hist_ref,
+    path_ref,
     low_ref,
     slot_ref,
     high_ref,
     piece_ref,
-    sems,
 ):
     groups = node_ref.shape[0]
     steps = groups // SUB
@@ -45,26 +36,7 @@
     nodes3 = f3_ref.shape[0]
     nodes4 = f4_ref.shape[0]
     tag_count = 2 * nodes4
-    moves = [
-        pltpu.make_async_copy(source, target, sems.at[i])
-        for i, (source, target) in enumerate(
-            (
-                (codes_hbm, codes_ref),
-                (node_hbm, node_ref),
-                (f3_hbm, f3_ref),
-                (b3_hbm, b3_ref),
-                (f4_hbm, f4_ref),
-                (b4_hbm, b4_ref),
-                (label_hbm, label_ref),
-                (weight_hbm, weight_ref),
-            )
-        )
-    ]
-    for move in moves:
-        move.start()
     piece_ref[...] = jnp.zeros_like(piece_ref)
-    for move in moves:
-        move.wait()
 
     def code_start(feature):
         return (feature // SUB) * (groups * SUB) + feature % SUB
@@ -315,22 +287,13 @@
     hist, path = pl.pallas_call(
         grow_kernel,
         out_shape=(pltpu.VMEM((hist_rows, LANES), f32), pltpu.VMEM(square, i32)),
-        in_specs=[whole(pltpu.HBM)] * 8,
+        in_specs=[whole(pltpu.SMEM)] * 4 + [whole()] * 4,
         out_specs=(whole(), whole()),
         scratch_shapes=[
-            pltpu.SMEM((nodes3,), i32),
-            pltpu.SMEM((nodes3,), i32),
-            pltpu.SMEM((nodes4,), i32),
-            pltpu.SMEM((nodes4,), i32),
-            pltpu.VMEM(codes.shape, i32),
-            pltpu.VMEM(square, i32),
-            pltpu.VMEM(square, f32),
-            pltpu.VMEM(square, f32),
             pltpu.VMEM((own, *square), i32),
             pltpu.VMEM((own, *square), i32),
             pltpu.VMEM(square, f32),
             pltpu.VMEM((groups * SUB, LANES), f32),
-            pltpu.SemaphoreType.DMA((8,)),
         ],
         compiler_params=pltpu.CompilerParams(vmem_limit_bytes=24 * 1024 * 1024),
     )(

time: 25.3 us -> 25.2 us (level)
  no operation moved by 1% of the time
where the time goes in v5:
time: 25.2 us; the launch traced here: 24.9 us
  waiting for transfers between devices  8.98 us (36%)
  starting transfers between devices  8.21 us (33%)
  Pallas kernels  6.92 us (27%)
  between operations  0.67 us (3%)
    ppermute x3, waiting for transfers between devices, combine_rows(): part = part + lax.ppermute(part, ('rows', 'feat'), pairs)  8.98 us
    ppermute x3, starting transfers between devices, combine_rows(): part = part + lax.ppermute(part, ('rows', 'feat'), pairs)  8.21 us
    pallas_call x1, Pallas kernels, on_device(): pl.pallas_call(grow_kernel, out_shape=(pltpu.VMEM((hist_rows, LANES), f32...  5.91 us
    pallas_call x1, Pallas kernels, on_device(): pl.pallas_call(functools.partial(finish_kernel, float(row_count * row_par...  1 us
  transfers between devices with their start and end apart: 3, of which 3 were waited for; matrix products, arithmetic and copies ran while one was open for 0% of the time, Pallas kernels for 0%

profile of v5, /device:TPU:0, one launch (start us, length us, event | category | flops | bytes accessed | tf_op | source)
XLA Modules:
  0.0 24.9 jit_solution(10411314321078235646)
XLA Ops:
  0.6 5.9 %shard_map.128 = (f32[264,128]{1,0:T(8,128)S(1)}, s32[120,128]{1,0:T(8,128)S(1)}) custom-call(s32[8]{0:T(128)} %f3_ref.1, s32[8]{0:T(128)} %b3_ref.1, s32[16]{0:T(128)} %f4_ref.1, s32[16]{0:T(128)} %b4_ref.1, s32[1920,128]{1,0:T(8,128)} %bitcast.15, s32[120,128]{1,0:T(8,128)} %bitcast.16, f32[120,128]{1,0:T(8,128)} %bitcast.17, f32[120,128]{1,0:T(8,128)} %bitcast.12), custom_call_target="tpu_custom_call" | custom-call | tf_op jit(solution)/shard_map/pallas_call | solution.py:287
  6.5 3.0 %collective-permute-start = (f32[264,128]{1,0:T(8,128)S(1)}, f32[264,128]{1,0:T(8,128)S(1)}, u32[]{:S(2)}, u32[]{:S(2)}) collective-permute-start(f32[264,128]{1,0:T(8,128)S(1)} %get-tuple-element.12), channel_id=1, source_target_pairs={{0,4},{1,17},{2,6},{3,19},{4,0},{5,21},{6,2},{7,23},{8,12},{9,25},... | collective-permute-start | bytes 405512 | tf_op jit(solution)/shard_map/ppermute | solution.py:242
  9.5 3.0 %collective-permute-done = f32[264,128]{1,0:T(8,128)S(1)} collective-permute-done((f32[264,128]{1,0:T(8,128)S(1)}, f32[264,128]{1,0:T(8,128)S(1)}, u32[]{:S(2)}, u32[]{:S(2)}) %collective-permute-start) | collective-permute-done | bytes 135200 | tf_op jit(solution)/shard_map/ppermute | solution.py:242
  12.5 2.1 %collective-permute-start.1 = (f32[264,128]{1,0:T(8,128)S(1)}, f32[264,128]{1,0:T(8,128)S(1)}, u32[]{:S(2)}, u32[]{:S(2)}) collective-permute-start(f32[264,128]{1,0:T(8,128)S(1)} %add.9), channel_id=1, source_target_pairs={{0,8},{1,5},{2,10},{3,7},{4,12},{5,1},{6,14},{7,3},{8,0},{9,13},{1... | collective-permute-start | bytes 405512 | tf_op jit(solution)/shard_map/ppermute | solution.py:242
  14.7 3.0 %collective-permute-done.1 = f32[264,128]{1,0:T(8,128)S(1)} collective-permute-done((f32[264,128]{1,0:T(8,128)S(1)}, f32[264,128]{1,0:T(8,128)S(1)}, u32[]{:S(2)}, u32[]{:S(2)}) %collective-permute-start.1) | collective-permute-done | bytes 135200 | tf_op jit(solution)/shard_map/ppermute | solution.py:242
  17.7 0.0 copy-start
  17.7 0.0 copy-start.1
  17.7 3.1 %collective-permute-start.2 = (f32[264,128]{1,0:T(8,128)S(1)}, f32[264,128]{1,0:T(8,128)S(1)}, u32[]{:S(2)}, u32[]{:S(2)}) collective-permute-start(f32[264,128]{1,0:T(8,128)S(1)} %add.10), channel_id=1, source_target_pairs={{0,16},{1,9},{2,18},{3,11},{4,20},{5,13},{6,22},{7,15},{8,24},{9,1... | collective-permute-start | bytes 405512 | tf_op jit(solution)/shard_map/ppermute | solution.py:242
  20.8 3.0 %collective-permute-done.2 = f32[264,128]{1,0:T(8,128)S(1)} collective-permute-done((f32[264,128]{1,0:T(8,128)S(1)}, f32[264,128]{1,0:T(8,128)S(1)}, u32[]{:S(2)}, u32[]{:S(2)}) %collective-permute-start.2) | collective-permute-done | bytes 135200 | tf_op jit(solution)/shard_map/ppermute | solution.py:242
  23.8 0.0 copy-done
  23.8 0.0 copy-done.1
  23.8 1.0 %shard_map.129 = (f32[4,16,256]{2,1,0:T(8,128)}, f32[4,32,256]{2,1,0:T(8,128)}, f32[1,32]{1,0:T(1,128)}, f32[120,128]{1,0:T(8,128)}, f32[120,128]{1,0:T(8,128)}) custom-call(f32[264,128]{1,0:T(8,128)S(1)} %add.11.hist_ref, s32[120,128]{1,0:T(8,128)S(1)} %get-tuple-element.13.path_ref, f32[120,128]{1,0:T(8,128)S(1)} %bitcast.13, f32[120,128]{1,0:T(8,128)S(1)} %bitcast.14), custom_call_target="tpu_custom_call" | custom-call | tf_op jit(solution)/shard_map/pallas_call | solution.py:310
  (3 shorter events, 0.1 us)
Async XLA Ops:
  6.5 6.0 %collective-permute-start = (f32[264,128]{1,0:T(8,128)S(1)}, f32[264,128]{1,0:T(8,128)S(1)}, u32[]{:S(2)}, u32[]{:S(2)}) collective-permute-start(f32[264,128]{1,0:T(8,128)S(1)} %get-tuple-element.12), channel_id=1, source_target_pairs={{0,4},{1,17},{2,6},{3,19},{4,0},{5,21},{6,2},{7,23},{8,12},{9,25},... | collective-permute-start | bytes 405512 | tf_op jit(solution)/shard_map/ppermute | solution.py:242
  12.5 5.1 %collective-permute-start.1 = (f32[264,128]{1,0:T(8,128)S(1)}, f32[264,128]{1,0:T(8,128)S(1)}, u32[]{:S(2)}, u32[]{:S(2)}) collective-permute-start(f32[264,128]{1,0:T(8,128)S(1)} %add.9), channel_id=1, source_target_pairs={{0,8},{1,5},{2,10},{3,7},{4,12},{5,1},{6,14},{7,3},{8,0},{9,13},{1... | collective-permute-start | bytes 405512 | tf_op jit(solution)/shard_map/ppermute | solution.py:242
  17.7 6.1 %copy-start = (f32[15360]{0:T(1024)S(1)}, f32[15360]{0:T(1024)}, u32[]{:S(2)}) copy-start(f32[15360]{0:T(1024)} %param.12) | copy-start | bytes 184324
  17.7 6.1 %copy-start.1 = (f32[15360]{0:T(1024)S(1)}, f32[15360]{0:T(1024)}, u32[]{:S(2)}) copy-start(f32[15360]{0:T(1024)} %param.13) | copy-start | bytes 184324
  17.7 6.1 %collective-permute-start.2 = (f32[264,128]{1,0:T(8,128)S(1)}, f32[264,128]{1,0:T(8,128)S(1)}, u32[]{:S(2)}, u32[]{:S(2)}) collective-permute-start(f32[264,128]{1,0:T(8,128)S(1)} %add.10), channel_id=1, source_target_pairs={{0,16},{1,9},{2,18},{3,11},{4,20},{5,13},{6,22},{7,15},{8,24},{9,1... | collective-permute-start | bytes 405512 | tf_op jit(solution)/shard_map/ppermute | solution.py:242

commit v6 on v5

--- a/solution.py
+++ b/solution.py
@@ -154,7 +154,8 @@
 
 def finish_kernel(
     total,
-    hist_ref,
+    part_ref,
+    received_ref,
     path_ref,
     weight_ref,
     score_ref,
@@ -169,8 +170,13 @@
     nodes4 = tags // 2
     nodes3 = nodes4 // 2
     leaves = value_ref.shape[1]
+
+    def hist_rows(first, count):
+        rows = slice(first, first + count)
+        return part_ref[rows, :] + received_ref[rows, :]
+
     for pair in range(own // 2):
-        turned = hist_ref[pair * LANES : (pair + 1) * LANES, :].T
+        turned = hist_rows(pair * LANES, LANES).T
         for q in range(4):
             i = 2 * pair + q // 2
             h = q % 2
@@ -191,7 +197,7 @@
                 weave_ref[pl.ds(keep + nodes4 + r, nodes3, stride=2), :] = diffs[r]
             hist4_ref[i, :, lanes] = weave_ref[keep : keep + tags, :]
     leaf_base = own // 2 * LANES
-    pieces = hist_ref[leaf_base : leaf_base + SUB, :]
+    pieces = hist_rows(leaf_base, SUB)
     lane = lax.broadcasted_iota(jnp.int32, (1, LANES), 1)
     right = (lane & tags) > 0
     positive = (lane & nodes3) > 0
@@ -231,7 +237,7 @@
 
 def combine_rows(part, row_parts, feat_parts):
     if row_parts & (row_parts - 1):
-        return lax.psum(part, "rows")
+        return lax.psum(part, "rows"), jnp.zeros_like(part)
     bits = row_parts.bit_length() - 1
     for step in range(bits):
         pairs = []
@@ -239,8 +245,11 @@
             for feat in range(feat_parts):
                 other = row ^ reach(feat, step, bits)
                 pairs.append((row * feat_parts + feat, other * feat_parts + feat))
-        part = part + lax.ppermute(part, ("rows", "feat"), pairs)
-    return part
+        received = lax.ppermute(part, ("rows", "feat"), pairs)
+        if step == bits - 1:
+            return part, received
+        part = part + received
+    return part, jnp.zeros_like(part)
 
 
 def reach(feat, step, bits):
@@ -306,7 +315,7 @@
         held(label_sq),
         held(weight_sq),
     )
-    hist = combine_rows(hist, row_parts, feat_parts)
+    hist, received = combine_rows(hist, row_parts, feat_parts)
     hist3, hist4, values, new_scores, new_weights = pl.pallas_call(
         functools.partial(finish_kernel, float(row_count * row_parts)),
         out_shape=(
@@ -316,11 +325,11 @@
             jax.ShapeDtypeStruct(square, f32),
             jax.ShapeDtypeStruct(square, f32),
         ),
-        in_specs=[whole()] * 4,
+        in_specs=[whole()] * 5,
         out_specs=(whole(),) * 5,
         scratch_shapes=[pltpu.VMEM((own * 2 * tags, LANES), f32)],
         compiler_params=pltpu.CompilerParams(vmem_limit_bytes=24 * 1024 * 1024),
-    )(hist, path, weight_sq, score_sq)
+    )(hist, received, path, weight_sq, score_sq)
     return (
         hist3,
         hist4,

time: 25.2 us -> 25.2 us (level)
  no operation moved by 1% of the time
where the time goes in v6:
time: 25.2 us; the launch traced here: 24.8 us
  waiting for transfers between devices  8.98 us (36%)
  starting transfers between devices  8.21 us (33%)
  Pallas kernels  6.92 us (27%)
  between operations  0.66 us (3%)
    ppermute x3, waiting for transfers between devices, combine_rows(): received = lax.ppermute(part, ('rows', 'feat'), pairs)  8.98 us
    ppermute x3, starting transfers between devices, combine_rows(): received = lax.ppermute(part, ('rows', 'feat'), pairs)  8.21 us
    pallas_call x1, Pallas kernels, on_device(): pl.pallas_call(grow_kernel, out_shape=(pltpu.VMEM((hist_rows, LANES), f32...  5.91 us
    pallas_call x1, Pallas kernels, on_device(): pl.pallas_call(functools.partial(finish_kernel, float(row_count * row_par...  1 us
  transfers between devices with their start and end apart: 3, of which 3 were waited for; matrix products, arithmetic and copies ran while one was open for 0% of the time, Pallas kernels for 0%

profile of v6, /device:TPU:0, one launch (start us, length us, event | category | flops | bytes accessed | tf_op | source)
XLA Modules:
  0.0 24.8 jit_solution(3372698893853718240)
XLA Ops:
  0.6 5.9 %shard_map.128 = (f32[264,128]{1,0:T(8,128)S(1)}, s32[120,128]{1,0:T(8,128)S(1)}) custom-call(s32[8]{0:T(128)} %f3_ref.1, s32[8]{0:T(128)} %b3_ref.1, s32[16]{0:T(128)} %f4_ref.1, s32[16]{0:T(128)} %b4_ref.1, s32[1920,128]{1,0:T(8,128)} %bitcast.15, s32[120,128]{1,0:T(8,128)} %bitcast.16, f32[120,128]{1,0:T(8,128)} %bitcast.17, f32[120,128]{1,0:T(8,128)} %bitcast.12), custom_call_target="tpu_custom_call" | custom-call | tf_op jit(solution)/shard_map/pallas_call | solution.py:296
  6.5 3.0 %collective-permute-start = (f32[264,128]{1,0:T(8,128)S(1)}, f32[264,128]{1,0:T(8,128)S(1)}, u32[]{:S(2)}, u32[]{:S(2)}) collective-permute-start(f32[264,128]{1,0:T(8,128)S(1)} %get-tuple-element.12), channel_id=1, source_target_pairs={{0,4},{1,17},{2,6},{3,19},{4,0},{5,21},{6,2},{7,23},{8,12},{9,25},... | collective-permute-start | bytes 405512 | tf_op jit(solution)/shard_map/ppermute | solution.py:248
  9.5 3.0 %collective-permute-done = f32[264,128]{1,0:T(8,128)S(1)} collective-permute-done((f32[264,128]{1,0:T(8,128)S(1)}, f32[264,128]{1,0:T(8,128)S(1)}, u32[]{:S(2)}, u32[]{:S(2)}) %collective-permute-start) | collective-permute-done | bytes 135200 | tf_op jit(solution)/shard_map/ppermute | solution.py:248
  12.5 0.0 copy-start
  12.5 0.0 copy-start.1
  12.6 2.1 %collective-permute-start.1 = (f32[264,128]{1,0:T(8,128)S(1)}, f32[264,128]{1,0:T(8,128)S(1)}, u32[]{:S(2)}, u32[]{:S(2)}) collective-permute-start(f32[264,128]{1,0:T(8,128)S(1)} %add.6), channel_id=1, source_target_pairs={{0,8},{1,5},{2,10},{3,7},{4,12},{5,1},{6,14},{7,3},{8,0},{9,13},{1... | collective-permute-start | bytes 405512 | tf_op jit(solution)/shard_map/ppermute | solution.py:248
  14.7 3.0 %collective-permute-done.1 = f32[264,128]{1,0:T(8,128)S(1)} collective-permute-done((f32[264,128]{1,0:T(8,128)S(1)}, f32[264,128]{1,0:T(8,128)S(1)}, u32[]{:S(2)}, u32[]{:S(2)}) %collective-permute-start.1) | collective-permute-done | bytes 135200 | tf_op jit(solution)/shard_map/ppermute | solution.py:248
  17.7 3.1 %collective-permute-start.2 = (f32[264,128]{1,0:T(8,128)S(1)}, f32[264,128]{1,0:T(8,128)S(1)}, u32[]{:S(2)}, u32[]{:S(2)}) collective-permute-start(f32[264,128]{1,0:T(8,128)S(1)} %add.7.part_ref), channel_id=1, source_target_pairs={{0,16},{1,9},{2,18},{3,11},{4,20},{5,13},{6,22},{7,15},{8,24},{9,1... | collective-permute-start | bytes 405512 | tf_op jit(solution)/shard_map/ppermute | solution.py:248
  20.8 3.0 %collective-permute-done.2.received_ref = f32[264,128]{1,0:T(8,128)S(1)} collective-permute-done((f32[264,128]{1,0:T(8,128)S(1)}, f32[264,128]{1,0:T(8,128)S(1)}, u32[]{:S(2)}, u32[]{:S(2)}) %collective-permute-start.2) | collective-permute-done | bytes 135200 | tf_op jit(solution)/shard_map/ppermute | solution.py:248
  23.8 0.0 copy-done
  23.8 0.0 copy-done.1
  23.8 1.0 %shard_map.129 = (f32[4,16,256]{2,1,0:T(8,128)}, f32[4,32,256]{2,1,0:T(8,128)}, f32[1,32]{1,0:T(1,128)}, f32[120,128]{1,0:T(8,128)}, f32[120,128]{1,0:T(8,128)}) custom-call(f32[264,128]{1,0:T(8,128)S(1)} %add.7.part_ref, f32[264,128]{1,0:T(8,128)S(1)} %collective-permute-done.2.received_ref, s32[120,128]{1,0:T(8,128)S(1)} %get-tuple-element.13.path_ref, ...), custom_call_target="tpu_custom_call" | custom-call | tf_op jit(solution)/shard_map/pallas_call | solution.py:319
  (2 shorter events, 0.0 us)
Async XLA Ops:
  6.5 6.0 %collective-permute-start = (f32[264,128]{1,0:T(8,128)S(1)}, f32[264,128]{1,0:T(8,128)S(1)}, u32[]{:S(2)}, u32[]{:S(2)}) collective-permute-start(f32[264,128]{1,0:T(8,128)S(1)} %get-tuple-element.12), channel_id=1, source_target_pairs={{0,4},{1,17},{2,6},{3,19},{4,0},{5,21},{6,2},{7,23},{8,12},{9,25},... | collective-permute-start | bytes 405512 | tf_op jit(solution)/shard_map/ppermute | solution.py:248
  12.5 11.3 %copy-start = (f32[15360]{0:T(1024)S(1)}, f32[15360]{0:T(1024)}, u32[]{:S(2)}) copy-start(f32[15360]{0:T(1024)} %param.12) | copy-start | bytes 184324
  12.5 11.3 %copy-start.1 = (f32[15360]{0:T(1024)S(1)}, f32[15360]{0:T(1024)}, u32[]{:S(2)}) copy-start(f32[15360]{0:T(1024)} %param.13) | copy-start | bytes 184324
  12.6 5.1 %collective-permute-start.1 = (f32[264,128]{1,0:T(8,128)S(1)}, f32[264,128]{1,0:T(8,128)S(1)}, u32[]{:S(2)}, u32[]{:S(2)}) collective-permute-start(f32[264,128]{1,0:T(8,128)S(1)} %add.6), channel_id=1, source_target_pairs={{0,8},{1,5},{2,10},{3,7},{4,12},{5,1},{6,14},{7,3},{8,0},{9,13},{1... | collective-permute-start | bytes 405512 | tf_op jit(solution)/shard_map/ppermute | solution.py:248
  17.7 6.1 %collective-permute-start.2 = (f32[264,128]{1,0:T(8,128)S(1)}, f32[264,128]{1,0:T(8,128)S(1)}, u32[]{:S(2)}, u32[]{:S(2)}) collective-permute-start(f32[264,128]{1,0:T(8,128)S(1)} %add.7.part_ref), channel_id=1, source_target_pairs={{0,16},{1,9},{2,18},{3,11},{4,20},{5,13},{6,22},{7,15},{8,24},{9,1... | collective-permute-start | bytes 405512 | tf_op jit(solution)/shard_map/ppermute | solution.py:248
